TPU v7x, 128 devices: a whole 4x4x4 slice. The times are simulated.
128 devices in a mesh: row: 8 (over y, core), col: 16 (over x, z).
Axes of the slice: x: 4, y: 4, z: 4, core: 2. Of those that a mesh axis runs over, the one named last changes fastest.
Arguments:
- noise: bfloat16 [8192, 4096], P('row', 'col'), may hold values from -6 to 6
- latents: bfloat16 [16384, 4096], P('col', 'row'), may hold values from -12 to 12
Outputs:
- transported: bfloat16 [8192, 4096], P('row', 'col')
- row_potential: float32 [8192], P('row')
- col_potential: float32 [16384], P('col')
All inputs are finite; a program needn't handle non-finite values.
Results may differ from a plain program's by a relative error of at most 0.018.
Values may be sent and summed in bfloat16 or wider, within the bound.
No kernel may reach another device: no remote copies, remote signals or barrier semaphores. Data moves between devices by JAX's collectives and lax.ppermute only.
A program may use at most 64 MiB of HBM per device.

v0:
```python
import math

import jax
import jax.numpy as jnp
from jax import lax
from jax.sharding import PartitionSpec as P

ITERS = 3


epsilon = 0.01


def row_logsum(scores):
    high = lax.pmax(jnp.max(scores, axis=1), "col")
    total = lax.psum(jnp.sum(jnp.exp(scores - high[:, None]), axis=1), "col")
    return high + jnp.log(total)


def col_logsum(scores):
    high = lax.pmax(jnp.max(scores, axis=0), "row")
    total = lax.psum(jnp.sum(jnp.exp(scores - high[None, :]), axis=0), "row")
    return high + jnp.log(total)


def on_device(noise, latents):
    local_rows = noise.shape[0]
    whole_lat = lax.all_gather(latents, "row", axis=1, tiled=True)
    local_cols = whole_lat.shape[0]
    width = whole_lat.shape[1]
    cross = lax.dot_general(
        lax.all_gather(noise, "col", axis=1, tiled=True),
        whole_lat,
        (((1,), (1,)), ((), ())),
        preferred_element_type=jnp.float32,
    )
    logits = cross * (2.0 / (width * epsilon))
    noise_count = local_rows * lax.axis_size("row")
    latent_count = local_cols * lax.axis_size("col")
    col_potential = jnp.zeros((local_cols,), jnp.float32)
    row_potential = jnp.zeros((local_rows,), jnp.float32)
    for step in range(ITERS):
        row_potential = -math.log(noise_count) - row_logsum(logits + col_potential[None, :])
        col_potential = -math.log(latent_count) - col_logsum(logits + row_potential[:, None])
    plan = jnp.exp(logits + row_potential[:, None] + col_potential[None, :]).astype(jnp.bfloat16)
    mass = lax.psum(jnp.sum(plan.astype(jnp.float32), axis=1), "col")
    numerator = jnp.dot(plan, whole_lat, preferred_element_type=jnp.float32)
    shares = lax.psum_scatter(
        numerator.astype(jnp.bfloat16), "col", scatter_dimension=1, tiled=True
    ).astype(jnp.float32)
    transported = (shares / mass[:, None]).astype(jnp.bfloat16)
    return (transported, row_potential, col_potential)


def solution(mesh):
    in_specs = (P("row", "col"), P("col", "row"))
    out_specs = (P("row", "col"), P("row"), P("col"))
    return jax.shard_map(
        on_device, mesh=mesh, in_specs=in_specs, out_specs=out_specs, check_vma=False
    )
```

profile of v0, /device:TPU:0, one launch (start us, length us, event | category | flops | bytes accessed | tf_op | source)
XLA Modules:
  0.0 586.9 jit_solution(10740638094713270430)
XLA Ops:
  7.2 0.0 all-gather.5.cloned.1.call-start
  7.2 0.7 all-gather.5.cloned.1.call-update
  7.9 0.0 all-gather.3.cloned.1.call-start
  7.9 0.7 all-gather.3.cloned.1.call-update
  8.6 0.0 reduce-scatter.2.cloned.1.call-start
  8.7 53.2 %all-gather.5.cloned.1.call-done = bf16[1024,4096]{1,0:T(8,128)(2,1)} async-done(((bf16[1024,512]{1,0:T(8,128)(2,1)}), bf16[1024,4096]{1,0:T(8,128)(2,1)}) %all-gather.5.cloned.1.call-update) | async-done | bytes 8388624 | tf_op jit(solution)/shard_map/all_gather | solution.py:28
  61.9 80.8 %all-gather.3.cloned.1.call-done = bf16[1024,4096]{1,0:T(8,128)(2,1)} async-done(((bf16[1024,256]{1,0:T(8,128)(2,1)}), bf16[1024,4096]{1,0:T(8,128)(2,1)}) %all-gather.3.cloned.1.call-update) | async-done | bytes 8388624 | tf_op jit(solution)/shard_map/all_gather | solution.py:32
  142.7 15.0 %fusion = (f32[1024]{0:T(1024)S(1)}, f32[1024,1024]{0,1:T(8,128)}) fusion(bf16[1024,4096]{1,0:T(8,128)(2,1)} %all-gather.3.cloned.1.call-done, bf16[1024,4096]{1,0:T(8,128)(2,1)} %all-gather.5.cloned.1.call-done), kind=kOutput, calls=%fused_computation.22 | convolution fusion | flops 8592030720 | bytes 20975616 | tf_op jit(solution)/shard_map/dot_general | solution.py:31
  157.7 38.1 %pmax.42 = f32[1024]{0:T(1024)S(1)} all-reduce(f32[1024]{0:T(1024)S(1)} %get-tuple-element.3), channel_id=1, replica_groups=mesh['row'=8,'col'=16] {'col'}, use_global_device_ids=true, to_apply=%region_1.0 | all-reduce | flops 1024 | bytes 8192 | tf_op jit(solution)/shard_map/pmax | solution.py:15
  195.9 2.8 exponential_reduce_fusion.5
  198.7 35.5 %psum.49 = f32[1024]{0:T(1024)S(1)} all-reduce(f32[1024]{0:T(1024)S(1)} %exponential_reduce_fusion.5), channel_id=1, replica_groups=mesh['row'=8,'col'=16] {'col'}, use_global_device_ids=true, to_apply=%region_3.0 | all-reduce | flops 1024 | bytes 8192 | tf_op jit(solution)/shard_map/psum | solution.py:16
  234.2 2.5 add_reduce_fusion.3
  236.7 12.4 %pmax.43 = f32[1024]{0:T(1024)S(1)} all-reduce(f32[1024]{0:T(1024)S(1)} %add_reduce_fusion.3), channel_id=1, replica_groups=mesh['row'=8,'col'=16] {'row'}, use_global_device_ids=true, to_apply=%region_5.0 | all-reduce | flops 1024 | bytes 8192 | tf_op jit(solution)/shard_map/pmax | solution.py:21
  249.1 3.1 exponential_reduce_fusion.4
  252.2 12.4 %psum.50 = f32[1024]{0:T(1024)S(1)} all-reduce(f32[1024]{0:T(1024)S(1)} %exponential_reduce_fusion.4), channel_id=1, replica_groups=mesh['row'=8,'col'=16] {'row'}, use_global_device_ids=true, to_apply=%region_7.0 | all-reduce | flops 1024 | bytes 8192 | tf_op jit(solution)/shard_map/psum | solution.py:22
  264.6 2.5 add_reduce_fusion.2
  267.2 37.5 %pmax.44 = f32[1024]{0:T(1024)S(1)} all-reduce(f32[1024]{0:T(1024)S(1)} %add_reduce_fusion.2), channel_id=1, replica_groups=mesh['row'=8,'col'=16] {'col'}, use_global_device_ids=true, to_apply=%region_9.0 | all-reduce | flops 1024 | bytes 8192 | tf_op jit(solution)/shard_map/pmax | solution.py:15
  304.6 2.9 exponential_reduce_fusion.3
  307.6 35.5 %psum.51 = f32[1024]{0:T(1024)S(1)} all-reduce(f32[1024]{0:T(1024)S(1)} %exponential_reduce_fusion.3), channel_id=1, replica_groups=mesh['row'=8,'col'=16] {'col'}, use_global_device_ids=true, to_apply=%region_11.0 | all-reduce | flops 1024 | bytes 8192 | tf_op jit(solution)/shard_map/psum | solution.py:16
  343.1 2.5 add_reduce_fusion.1
  345.6 12.4 %pmax.45 = f32[1024]{0:T(1024)S(1)} all-reduce(f32[1024]{0:T(1024)S(1)} %add_reduce_fusion.1), channel_id=1, replica_groups=mesh['row'=8,'col'=16] {'row'}, use_global_device_ids=true, to_apply=%region_13.0 | all-reduce | flops 1024 | bytes 8192 | tf_op jit(solution)/shard_map/pmax | solution.py:21
  358.0 3.1 exponential_reduce_fusion.2
  361.1 12.4 %psum.52 = f32[1024]{0:T(1024)S(1)} all-reduce(f32[1024]{0:T(1024)S(1)} %exponential_reduce_fusion.2), channel_id=1, replica_groups=mesh['row'=8,'col'=16] {'row'}, use_global_device_ids=true, to_apply=%region_15.0 | all-reduce | flops 1024 | bytes 8192 | tf_op jit(solution)/shard_map/psum | solution.py:22
  373.6 2.5 add_reduce_fusion
  376.1 37.5 %pmax.46 = f32[1024]{0:T(1024)S(1)} all-reduce(f32[1024]{0:T(1024)S(1)} %add_reduce_fusion), channel_id=1, replica_groups=mesh['row'=8,'col'=16] {'col'}, use_global_device_ids=true, to_apply=%region_17.0 | all-reduce | flops 1024 | bytes 8192 | tf_op jit(solution)/shard_map/pmax | solution.py:15
  413.6 2.9 exponential_reduce_fusion.1
  416.5 35.5 %psum.53 = f32[1024]{0:T(1024)S(1)} all-reduce(f32[1024]{0:T(1024)S(1)} %exponential_reduce_fusion.1), channel_id=1, replica_groups=mesh['row'=8,'col'=16] {'col'}, use_global_device_ids=true, to_apply=%region_19.0 | all-reduce | flops 1024 | bytes 8192 | tf_op jit(solution)/shard_map/psum | solution.py:16
  452.0 0.0 copy-start
  452.0 2.5 add_reduce_fusion.4
  454.5 12.6 %pmax.47 = f32[1024]{0:T(1024)S(1)} all-reduce(f32[1024]{0:T(1024)S(1)} %add_reduce_fusion.4), channel_id=1, replica_groups=mesh['row'=8,'col'=16] {'row'}, use_global_device_ids=true, to_apply=%region_21.0 | all-reduce | flops 1024 | bytes 8192 | tf_op jit(solution)/shard_map/pmax | solution.py:21
  467.1 3.1 exponential_reduce_fusion
  470.2 12.4 %psum.54 = f32[1024]{0:T(1024)S(1)} all-reduce(f32[1024]{0:T(1024)S(1)} %exponential_reduce_fusion), channel_id=1, replica_groups=mesh['row'=8,'col'=16] {'row'}, use_global_device_ids=true, to_apply=%region_23.0 | all-reduce | flops 1024 | bytes 8192 | tf_op jit(solution)/shard_map/psum | solution.py:22
  482.6 0.0 copy-start.1
  482.6 15.0 %convolution_convert_fusion = bf16[1024,4096]{1,0:T(8,128)(2,1)} fusion(bf16[1024,4096]{1,0:T(8,128)(2,1)} %all-gather.5.cloned.1.call-done, f32[1024,1024]{0,1:T(8,128)} %get-tuple-element.4, f32[1024]{0:T(1024)S(1)} %add_subtract_fusion, f32[1024]{0:T(1024)S(1)} %add_subtract_fusion.1), kind=kOutput, calls=%fused_computation | convolution fusion | flops 8597274624 | bytes 20979712 | tf_op jit(solution)/shard_map/dot_general | solution.py:47
  497.6 0.0 reduce-scatter.2.cloned.1.call-update
  497.7 0.0 copy-done
  497.7 0.0 copy-done.1
  497.7 2.9 convert_reduce_fusion
  500.6 38.1 %psum.55 = f32[1024]{0:T(1024)S(1)} all-reduce(f32[1024]{0:T(1024)S(1)} %convert_reduce_fusion), channel_id=1, replica_groups=mesh['row'=8,'col'=16] {'col'}, use_global_device_ids=true, to_apply=%region_26.0 | all-reduce | flops 1024 | bytes 8192 | tf_op jit(solution)/shard_map/psum | solution.py:46
  538.7 39.5 %reduce-scatter.2.cloned.1.call-done = bf16[1024,256]{1,0:T(8,128)(2,1)} async-done(((bf16[1024,4096]{1,0:T(8,128)(2,1)}), bf16[1024,256]{1,0:T(8,128)(2,1)}) %reduce-scatter.2.cloned.1.call-update) | async-done | bytes 524304 | tf_op jit(solution)/shard_map/reduce_scatter | solution.py:48
  578.3 2.0 divide_convert_fusion
  (6 shorter events, 0.1 us)
Async XLA Ops:
  7.2 54.7 %all-gather.5.cloned.1.call-start = ((), (), s32[]{:S(2)}) async-start(), calls=%async_computation.2 | async-start | bytes 9437184 | tf_op jit(solution)/shard_map/all_gather | solution.py:28
  7.9 134.8 %all-gather.3.cloned.1.call-start = ((), (), s32[]{:S(2)}) async-start(), calls=%async_computation.1 | async-start | bytes 8912896 | tf_op jit(solution)/shard_map/all_gather | solution.py:32
  8.6 569.6 %reduce-scatter.2.cloned.1.call-start = ((), (), s32[]{:S(2)}) async-start(), calls=%async_computation.3 | async-start | bytes 8912896 | tf_op jit(solution)/shard_map/reduce_scatter | solution.py:48
  452.0 45.7 %copy-start = (f32[1024]{0:T(1024)}, f32[1024]{0:T(1024)S(1)}, u32[]{:S(2)}) copy-start(f32[1024]{0:T(1024)S(1)} %add_subtract_fusion.1) | copy-start | bytes 12292
  482.6 15.0 %copy-start.1 = (f32[1024]{0:T(1024)}, f32[1024]{0:T(1024)S(1)}, u32[]{:S(2)}) copy-start(f32[1024]{0:T(1024)S(1)} %add_subtract_fusion) | copy-start | bytes 12292
Sparse Core Ops, SparseCore 0:
  9.7 52.1 all-gather.4
  64.0 78.6 all-gather.2
  497.8 80.4 reduce-scatter.1
where the time goes:
time: 588 us; the launch traced here: 587 us
  blocking collectives  332 us (56%)
  waiting for transfers between devices  175 us (30%)
  other arithmetic  35.6 us (6%)
  matrix products  30 us (5%)
  between operations  13.8 us (2%)
    pmax x3, blocking collectives, row_logsum(): high = lax.pmax(jnp.max(scores, axis=1), 'col')  113 us
    psum x3, blocking collectives, row_logsum(): total = lax.psum(jnp.sum(jnp.exp(scores - high[:, None]), axis=1), 'col')  106 us
    all_gather x1, waiting for transfers between devices, on_device(): lax.all_gather(noise, 'col', axis=1, tiled=True)  80.8 us
    all_gather x1, waiting for transfers between devices, on_device(): whole_lat = lax.all_gather(latents, 'row', axis=1, tiled=True)  53.2 us
    reduce_scatter x1, waiting for transfers between devices, on_device(): lax.psum_scatter(numerator.astype(jnp.bfloat16), 'col', scatter_dimension...  39.5 us
    psum x1, blocking collectives, on_device(): mass = lax.psum(jnp.sum(plan.astype(jnp.float32), axis=1), 'col')  38.1 us
    pmax x3, blocking collectives, col_logsum(): high = lax.pmax(jnp.max(scores, axis=0), 'row')  37.4 us
    psum x3, blocking collectives, col_logsum(): total = lax.psum(jnp.sum(jnp.exp(scores - high[None, :]), axis=0), 'row')  37.3 us
  transfers between devices with their start and end apart: 3, of which 3 were waited for; matrix products, arithmetic and copies ran while one was open for 0% of the time, Pallas kernels for 0%

commit v1 on v0

v1 whole, which is shorter than its diff:
```python
import functools
import math

import jax
import jax.numpy as jnp
from jax import lax
from jax.experimental import pallas as pl
from jax.experimental.pallas import tpu as pltpu
from jax.sharding import PartitionSpec as P

ITERS = 3
EPSILON = 0.01
LOG2E = math.log2(math.e)
LN2 = math.log(2.0)
NX, NY, NZ, NC = 4, 4, 4, 2

F32 = jnp.float32
BF16 = jnp.bfloat16


def shift_z(by):
    return [(x * NZ + z, x * NZ + (z + by) % NZ) for x in range(NX) for z in range(NZ)]


def shift_x(by):
    return [(x * NZ + z, (x + by) % NX * NZ + z) for x in range(NX) for z in range(NZ)]


def shift_y(by):
    return [(y * NC + c, (y + by) % NY * NC + c) for y in range(NY) for c in range(NC)]


def swap_core():
    return [(y * NC + c, y * NC + 1 - c) for y in range(NY) for c in range(NC)]


def logadd(parts):
    high = functools.reduce(jnp.maximum, parts)
    total = functools.reduce(jnp.add, [jnp.exp2(p - high) for p in parts])
    return high + jnp.log2(total)


def over(value, axis, perms, combine):
    return combine([value] + [lax.ppermute(value, axis, p) for p in perms])


def over_col(value, combine):
    value = over(value, "col", [shift_z(b) for b in (1, 3, 2)], combine)
    return over(value, "col", [shift_x(b) for b in (1, 3, 2)], combine)


def over_row(value, combine):
    value = over(value, "row", [swap_core()], combine)
    return over(value, "row", [shift_y(b) for b in (1, 3, 2)], combine)


def eye():
    return lax.broadcasted_iota(jnp.int32, (128, 128), 0) == lax.broadcasted_iota(
        jnp.int32, (128, 128), 1
    )


def to_lanes(column):
    mask = eye()
    return jnp.concatenate(
        [
            jnp.sum(jnp.where(mask, column[at : at + 128], 0.0), axis=0, keepdims=True)
            for at in range(0, column.shape[0], 128)
        ],
        axis=1,
    )


def to_sublanes(line):
    mask = eye()
    return jnp.concatenate(
        [
            jnp.sum(jnp.where(mask, line[:, at : at + 128], 0.0), axis=1, keepdims=True)
            for at in range(0, line.shape[1], 128)
        ],
        axis=0,
    )


def row_lse_block(read, rows, out):
    step = 32
    columns = []
    for at in range(0, rows, step):
        t = read(at, step)
        high = jnp.max(t, axis=1, keepdims=True)
        total = jnp.sum(jnp.exp2(t - high), axis=1, keepdims=True)
        columns.append(high + jnp.log2(total))
    out[...] = to_lanes(jnp.concatenate(columns, axis=0))


def cross_kernel(scale, noise_ref, lat_ref, logits_ref, lse_ref):
    cross = lax.dot_general(
        noise_ref[...], lat_ref[...], (((1,), (1,)), ((), ())), preferred_element_type=F32
    )
    logits_ref[...] = cross * scale
    row_lse_block(lambda at, n: logits_ref[pl.ds(at, n), :], noise_ref.shape[0], lse_ref)


def cross_call(noise, lat, scale):
    rows, width = noise.shape
    cols = lat.shape[0]
    block = 256
    return pl.pallas_call(
        functools.partial(cross_kernel, scale),
        grid=(rows // block,),
        in_specs=[
            pl.BlockSpec((block, width), lambda i: (i, 0)),
            pl.BlockSpec((cols, width), lambda i: (0, 0)),
        ],
        out_specs=[
            pl.BlockSpec((block, cols), lambda i: (i, 0)),
            pl.BlockSpec((1, block), lambda i: (0, i)),
        ],
        out_shape=[
            jax.ShapeDtypeStruct((rows, cols), F32),
            jax.ShapeDtypeStruct((1, rows), F32),
        ],
        compiler_params=pltpu.CompilerParams(vmem_limit_bytes=40 * 2**20),
        name="cross",
    )(noise, lat)


def row_kernel(logits_ref, colpot_ref, lse_ref):
    colpot = colpot_ref[...]
    row_lse_block(
        lambda at, n: logits_ref[pl.ds(at, n), :] + colpot, logits_ref.shape[0], lse_ref
    )


def row_call(logits, colpot):
    rows, cols = logits.shape
    block = 256
    return pl.pallas_call(
        row_kernel,
        grid=(rows // block,),
        in_specs=[
            pl.BlockSpec((block, cols), lambda i: (i, 0)),
            pl.BlockSpec((1, cols), lambda i: (0, 0)),
        ],
        out_specs=pl.BlockSpec((1, block), lambda i: (0, i)),
        out_shape=jax.ShapeDtypeStruct((1, rows), F32),
        compiler_params=pltpu.CompilerParams(vmem_limit_bytes=16 * 2**20),
        name="row_lse",
    )(logits, colpot)


def col_kernel(logits_ref, rowpot_ref, lse_ref, part_ref):
    step = pl.program_id(0)
    rows, cols = logits_ref.shape
    rowpot = jnp.broadcast_to(to_sublanes(rowpot_ref[...]), (rows, 128))
    lines = []
    for at in range(0, cols, 128):
        t = logits_ref[:, pl.ds(at, 128)] + rowpot
        high = jnp.max(t, axis=0, keepdims=True)
        total = jnp.sum(jnp.exp2(t - high), axis=0, keepdims=True)
        lines.append(high + jnp.log2(total))
    part_ref[pl.ds(step, 1), :] = jnp.concatenate(lines, axis=1)

    @pl.when(step == pl.num_programs(0) - 1)
    def finish():
        parts = part_ref[...]
        high = jnp.max(parts, axis=0, keepdims=True)
        total = jnp.sum(jnp.exp2(parts - high), axis=0, keepdims=True)
        lse_ref[...] = high + jnp.log2(total)


def col_call(logits, rowpot):
    rows, cols = logits.shape
    block = 256
    return pl.pallas_call(
        col_kernel,
        grid=(rows // block,),
        in_specs=[
            pl.BlockSpec((block, cols), lambda i: (i, 0)),
            pl.BlockSpec((1, block), lambda i: (0, i)),
        ],
        out_specs=pl.BlockSpec((1, cols), lambda i: (0, 0)),
        out_shape=jax.ShapeDtypeStruct((1, cols), F32),
        scratch_shapes=[pltpu.VMEM((rows // block, cols), F32)],
        compiler_params=pltpu.CompilerParams(vmem_limit_bytes=16 * 2**20),
        name="col_lse",
    )(logits, rowpot)


def plan_kernel(logits_ref, rowpot_ref, colpot_ref, lat_ref, share_ref, mass_ref):
    rowpot = to_sublanes(rowpot_ref[...])
    plan = jnp.exp2(logits_ref[...] + rowpot + colpot_ref[...]).astype(BF16)
    mass_ref[...] = to_lanes(jnp.sum(plan.astype(F32), axis=1, keepdims=True))
    share_ref[...] = jnp.dot(plan, lat_ref[...], preferred_element_type=F32).astype(BF16)


def plan_call(logits, rowpot, colpot, lat):
    rows, cols = logits.shape
    width = lat.shape[1]
    block = 256
    return pl.pallas_call(
        plan_kernel,
        grid=(rows // block,),
        in_specs=[
            pl.BlockSpec((block, cols), lambda i: (i, 0)),
            pl.BlockSpec((1, block), lambda i: (0, i)),
            pl.BlockSpec((1, cols), lambda i: (0, 0)),
            pl.BlockSpec((cols, width), lambda i: (0, 0)),
        ],
        out_specs=[
            pl.BlockSpec((block, width), lambda i: (i, 0)),
            pl.BlockSpec((1, block), lambda i: (0, i)),
        ],
        out_shape=[
            jax.ShapeDtypeStruct((rows, width), BF16),
            jax.ShapeDtypeStruct((1, rows), F32),
        ],
        compiler_params=pltpu.CompilerParams(vmem_limit_bytes=48 * 2**20),
        name="plan",
    )(logits, rowpot, colpot, lat)


def on_device(noise, latents):
    whole_lat = lax.all_gather(latents, "row", axis=1, tiled=True)
    whole_noise = lax.all_gather(noise, "col", axis=1, tiled=True)
    width = whole_lat.shape[1]
    noise_count = noise.shape[0] * lax.axis_size("row")
    latent_count = latents.shape[0] * lax.axis_size("col")
    logits, lse = cross_call(whole_noise, whole_lat, 2.0 / (width * EPSILON) * LOG2E)
    for step in range(ITERS):
        if step:
            lse = row_call(logits, colpot)
        rowpot = -math.log2(noise_count) - over_col(lse, logadd)
        colpot = -math.log2(latent_count) - over_row(col_call(logits, rowpot), logadd)
    share, mass = plan_call(logits, rowpot, colpot, whole_lat)
    mass = over_col(mass, lambda parts: functools.reduce(jnp.add, parts))
    total = lax.psum_scatter(share, "col", scatter_dimension=1, tiled=True).astype(F32)
    transported = (total / mass.reshape(-1, 1)).astype(BF16)
    return (transported, rowpot.reshape(-1) * LN2, colpot.reshape(-1) * LN2)


def solution(mesh):
    in_specs = (P("row", "col"), P("col", "row"))
    out_specs = (P("row", "col"), P("row"), P("col"))
    return jax.shard_map(
        on_device, mesh=mesh, in_specs=in_specs, out_specs=out_specs, check_vma=False
    )
```

time: 588 us -> 346 us (0.59)
  blocking collectives: 332 us -> 0 us
  waiting for transfers between devices: 175 us -> 254 us
  Pallas kernels: 0 us -> 37.8 us
  starting transfers between devices: 0.11 us -> 32.9 us
  other arithmetic: 35.6 us -> 3.76 us
  matrix products: 30 us -> 0 us
    psum x7 -> x0, blocking collectives: 182 us -> none  [the longest x3 106 us: row_logsum(): total = lax.psum(jnp.sum(jnp.exp(scores - high[:, None]), axis=1), 'col')]
    pmax x6 -> x0, blocking collectives: 151 us -> none  [the longest x3 113 us: row_logsum(): high = lax.pmax(jnp.max(scores, axis=1), 'col')]
    ppermute x0 -> x36, waiting for transfers between devices: none -> 51.1 us  [over(): return combine([value] + [lax.ppermute(value, axis, p) for p in perms])]
    pallas_call x0 -> x7, Pallas kernels: none -> 37.8 us  [the longest x1 15.2 us: plan_call(): pl.pallas_call(plan_kernel, grid=(rows // block,), in_specs=[pl.BlockSpec...]
    ppermute x0 -> x36, starting transfers between devices: none -> 32.8 us  [over(): return combine([value] + [lax.ppermute(value, axis, p) for p in perms])]
    dot_general x2 -> x0, matrix products: 30 us -> none  [the longest x1 15 us: on_device(): lax.dot_general(lax.all_gather(noise, 'col', axis=1, tiled=True), whole_l...]
    reduce_scatter x1, waiting for transfers between devices: 39.5 us -> 67 us  [on_device(): lax.psum_scatter(share, 'col', scatter_dimension=1, tiled=True).astype(F32)]
    reduce_sum x7 -> x0, other arithmetic: 20.8 us -> none  [the longest x3 9.19 us: col_logsum(): total = lax.psum(jnp.sum(jnp.exp(scores - high[None, :]), axis=0), 'row')]
  transfers between devices with their start and end apart: 3 -> 39, of which waited for: 3 -> 29; matrix products, arithmetic and copies ran while one was open for 0% -> 0% of each run, Pallas kernels for 0% -> 0%
where the time goes in v1:
time: 346 us; the launch traced here: 345 us
  waiting for transfers between devices  254 us (73%)
  Pallas kernels  37.8 us (11%)
  starting transfers between devices  32.9 us (10%)
  between operations  13.9 us (4%)
  other arithmetic  3.76 us (1%)
    all_gather x1, waiting for transfers between devices, on_device(): whole_noise = lax.all_gather(noise, 'col', axis=1, tiled=True)  80.8 us
    reduce_scatter x1, waiting for transfers between devices, on_device(): lax.psum_scatter(share, 'col', scatter_dimension=1, tiled=True).astype(F32)  67 us
    all_gather x1, waiting for transfers between devices, on_device(): whole_lat = lax.all_gather(latents, 'row', axis=1, tiled=True)  53.2 us
    ppermute x36, waiting for transfers between devices, over(): return combine([value] + [lax.ppermute(value, axis, p) for p in perms])  51.1 us
    ppermute x36, starting transfers between devices, over(): return combine([value] + [lax.ppermute(value, axis, p) for p in perms])  32.8 us
    pallas_call x1, Pallas kernels, plan_call(): pl.pallas_call(plan_kernel, grid=(rows // block,), in_specs=[pl.BlockSpec...  15.2 us
    pallas_call x1, Pallas kernels, cross_call(): pl.pallas_call(functools.partial(cross_kernel, scale), grid=(rows // bloc...  14.2 us
  transfers between devices with their start and end apart: 39, of which 29 were waited for; matrix products, arithmetic and copies ran while one was open for 0% of the time, Pallas kernels for 0%

profile of v1, /device:TPU:0, one launch (start us, length us, event | category | flops | bytes accessed | tf_op | source)
XLA Modules:
  0.0 345.3 jit_solution(1113634451252743760)
XLA Ops:
  7.2 0.7 all-gather.5.cloned.1.call-update
  7.9 0.7 all-gather.3.cloned.1.call-update
  8.7 53.2 %all-gather.5.cloned.1.call-done.lat_ref = bf16[1024,4096]{1,0:T(8,128)(2,1)} async-done(((bf16[1024,512]{1,0:T(8,128)(2,1)}), bf16[1024,4096]{1,0:T(8,128)(2,1)}) %all-gather.5.cloned.1.call-update) | async-done | bytes 8388624 | tf_op jit(solution)/shard_map/all_gather | solution.py:224
  61.9 80.8 %all-gather.3.cloned.1.call-done.noise_ref = bf16[1024,4096]{1,0:T(8,128)(2,1)} async-done(((bf16[1024,256]{1,0:T(8,128)(2,1)}), bf16[1024,4096]{1,0:T(8,128)(2,1)}) %all-gather.3.cloned.1.call-update) | async-done | bytes 8388624 | tf_op jit(solution)/shard_map/all_gather | solution.py:225
  142.7 3.4 copy-done
  146.1 14.2 %cross.1 = (f32[1024,1024]{1,0:T(8,128)S(1)}, f32[1,1024]{1,0:T(1,128)S(1)}) custom-call(bf16[1024,4096]{1,0:T(8,128)(2,1)S(1)} %copy-done, bf16[1024,4096]{1,0:T(8,128)(2,1)} %all-gather.5.cloned.1.call-done.lat_ref), custom_call_target="tpu_custom_call" | custom-call | tf_op jit(solution)/shard_map/cross/pallas_call | solution.py:108
  160.3 1.6 collective-permute-start.2
  161.9 2.3 collective-permute-start.1
  164.2 1.3 collective-permute-done.2
  165.5 3.5 %collective-permute-done = f32[1,1024]{1,0:T(1,128)S(1)} collective-permute-done((f32[1,1024]{1,0:T(1,128)S(1)}, f32[1,1024]{1,0:T(1,128)S(1)}, u32[]{:S(2)}, u32[]{:S(2)}) %collective-permute-start) | collective-permute-done | bytes 4128 | tf_op jit(solution)/shard_map/ppermute | solution.py:44
  169.0 1.5 collective-permute-start.5
  170.6 1.5 collective-permute-start.4
  172.1 0.6 collective-permute-start.3
  172.6 1.6 collective-permute-done.5
  174.2 2.6 collective-permute-done.3
  176.9 1.7 col_lse.3
  178.7 1.2 collective-permute-done.6
  179.9 3.1 collective-permute-start.9
  183.0 1.1 collective-permute-start.8
  184.1 0.9 collective-permute-start.7
  185.1 1.5 collective-permute-done.8
  186.6 2.4 collective-permute-done.7
  189.0 1.7 row_lse.2
  191.1 1.8 collective-permute-start.11
  193.1 2.8 collective-permute-done.12
  195.9 1.8 collective-permute-done.10
  198.1 2.0 collective-permute-start.14
  200.1 2.8 collective-permute-done.15
  202.9 2.0 collective-permute-done.13
  205.0 1.7 col_lse.4
  206.8 1.2 collective-permute-done.16
  208.3 2.0 collective-permute-start.18
  210.4 2.8 collective-permute-done.19
  213.1 2.0 collective-permute-done.17
  215.2 1.7 row_lse.3
  217.0 1.5 collective-permute-start.21
  218.5 0.6 collective-permute-start.20
  219.1 3.0 collective-permute-done.22
  222.1 1.2 collective-permute-done.20
  223.7 1.2 collective-permute-start.24
  224.9 0.8 collective-permute-start.23
  225.7 2.8 collective-permute-done.25
  228.5 1.2 collective-permute-done.23
  229.8 0.6 broadcast_multiply_fusion
  230.4 1.7 col_lse.5
  232.2 1.2 collective-permute-done.26
  233.5 1.5 collective-permute-start.28
  234.9 0.6 collective-permute-start.27
  235.6 3.0 collective-permute-done.29
  238.6 1.2 collective-permute-done.27
  239.7 0.6 broadcast_multiply_fusion.1
  240.4 15.2 %plan.1 = (bf16[1024,4096]{1,0:T(8,128)(2,1)}, f32[1,1024]{1,0:T(1,128)S(1)}) custom-call(f32[1024,1024]{1,0:T(8,128)S(1)} %get-tuple-element.7.logits_ref, f32[1,1024]{1,0:T(1,128)S(1)} %get-tuple-element.14.rowpot_ref, f32[1,1024]{1,0:T(1,128)S(1)} %get-tuple-element.12.colpot_ref, bf16[1024,4096]{1,0:T(8,128)(2,1)} %all-gather.5.cloned.1.call-done.lat_ref), custom_call_target="tpu_custom_call" | custom-call | tf_op jit(solution)/shard_map/plan/pallas_call | solution.py:201
  255.6 1.0 collective-permute-start.32
  256.6 1.2 collective-permute-start.31
  257.8 0.8 collective-permute-start.30
  258.6 2.1 collective-permute-done.32
  260.8 1.9 collective-permute-done.30
  262.7 1.0 collective-permute-start.35
  263.6 1.2 collective-permute-start.34
  264.8 0.8 collective-permute-start.33
  265.6 2.2 collective-permute-done.35
  267.9 1.8 collective-permute-done.33
  269.7 67.0 %reduce-scatter.2.cloned.1.call-done = bf16[1024,256]{1,0:T(8,128)(2,1)} async-done(((bf16[1024,4096]{1,0:T(8,128)(2,1)}), bf16[1024,256]{1,0:T(8,128)(2,1)}) %reduce-scatter.2.cloned.1.call-update) | async-done | bytes 524304 | tf_op jit(solution)/shard_map/reduce_scatter | solution.py:237
  336.7 2.0 divide_convert_fusion
  (41 shorter events, 2.8 us)
Async XLA Ops:
  7.2 54.7 %all-gather.5.cloned.1.call-start = ((), (), s32[]{:S(2)}) async-start(), calls=%async_computation.2 | async-start | bytes 9437184 | tf_op jit(solution)/shard_map/all_gather | solution.py:224
  7.9 134.8 %all-gather.3.cloned.1.call-start = ((), (), s32[]{:S(2)}) async-start(), calls=%async_computation.1 | async-start | bytes 8912896 | tf_op jit(solution)/shard_map/all_gather | solution.py:225
  8.6 328.1 %reduce-scatter.2.cloned.1.call-start = ((), (), s32[]{:S(2)}) async-start(), calls=%async_computation.3 | async-start | bytes 8912896 | tf_op jit(solution)/shard_map/reduce_scatter | solution.py:237
  142.7 3.4 copy-start
  160.3 5.2 %collective-permute-start.2 = (f32[1,1024]{1,0:T(1,128)S(1)}, f32[1,1024]{1,0:T(1,128)S(1)}, u32[]{:S(2)}, u32[]{:S(2)}) collective-permute-start(f32[1,1024]{1,0:T(1,128)S(1)} %get-tuple-element.8), channel_id=1, source_target_pairs={{0,2},{1,3},{2,0},{3,1},{4,6},{5,7},{6,4},{7,5},{8,10},{9,11},{10,... | collective-permute-start | bytes 12296 | tf_op jit(solution)/shard_map/ppermute | solution.py:44
  161.9 3.6 %collective-permute-start.1 = (f32[1,1024]{1,0:T(1,128)S(1)}, f32[1,1024]{1,0:T(1,128)S(1)}, u32[]{:S(2)}, u32[]{:S(2)}) collective-permute-start(f32[1,1024]{1,0:T(1,128)S(1)} %get-tuple-element.8), channel_id=1, source_target_pairs={{0,3},{1,0},{2,1},{3,2},{4,7},{5,4},{6,5},{7,6},{8,11},{9,8},{10,9... | collective-permute-start | bytes 12296 | tf_op jit(solution)/shard_map/ppermute | solution.py:44
  164.2 4.8 %collective-permute-start = (f32[1,1024]{1,0:T(1,128)S(1)}, f32[1,1024]{1,0:T(1,128)S(1)}, u32[]{:S(2)}, u32[]{:S(2)}) collective-permute-start(f32[1,1024]{1,0:T(1,128)S(1)} %get-tuple-element.8), channel_id=1, source_target_pairs={{0,1},{1,2},{2,3},{3,0},{4,5},{5,6},{6,7},{7,4},{8,9},{9,10},{10,1... | collective-permute-start | bytes 12296 | tf_op jit(solution)/shard_map/ppermute | solution.py:44
  169.0 5.2 %collective-permute-start.5 = (f32[1,1024]{1,0:T(1,128)S(1)}, f32[1,1024]{1,0:T(1,128)S(1)}, u32[]{:S(2)}, u32[]{:S(2)}) collective-permute-start(f32[1,1024]{1,0:T(1,128)S(1)} %multiply_add_fusion.5), channel_id=1, source_target_pairs={{0,8},{1,9},{2,10},{3,11},{4,12},{5,13},{6,14},{7,15},{8,0},{9,1},... | collective-permute-start | bytes 12296 | tf_op jit(solution)/shard_map/ppermute | solution.py:44
  170.6 3.6 %collective-permute-start.4 = (f32[1,1024]{1,0:T(1,128)S(1)}, f32[1,1024]{1,0:T(1,128)S(1)}, u32[]{:S(2)}, u32[]{:S(2)}) collective-permute-start(f32[1,1024]{1,0:T(1,128)S(1)} %multiply_add_fusion.5), channel_id=1, source_target_pairs={{0,12},{1,13},{2,14},{3,15},{4,0},{5,1},{6,2},{7,3},{8,4},{9,5},{1... | collective-permute-start | bytes 12296 | tf_op jit(solution)/shard_map/ppermute | solution.py:44
  172.1 4.8 %collective-permute-start.3 = (f32[1,1024]{1,0:T(1,128)S(1)}, f32[1,1024]{1,0:T(1,128)S(1)}, u32[]{:S(2)}, u32[]{:S(2)}) collective-permute-start(f32[1,1024]{1,0:T(1,128)S(1)} %multiply_add_fusion.5), channel_id=1, source_target_pairs={{0,4},{1,5},{2,6},{3,7},{4,8},{5,9},{6,10},{7,11},{8,12},{9,13},{1... | collective-permute-start | bytes 12296 | tf_op jit(solution)/shard_map/ppermute | solution.py:44
  178.6 1.2 collective-permute-start.6
  179.9 5.2 %collective-permute-start.9 = (f32[1,1024]{1,0:T(1,128)S(1)}, f32[1,1024]{1,0:T(1,128)S(1)}, u32[]{:S(2)}, u32[]{:S(2)}) collective-permute-start(f32[1,1024]{1,0:T(1,128)S(1)} %multiply_add_fusion.4), channel_id=1, source_target_pairs={{0,64},{16,80},{32,96},{48,112},{64,0},{80,16},{96,32},{112,48},{1... | collective-permute-start | bytes 12296 | tf_op jit(solution)/shard_map/ppermute | solution.py:44
  183.0 3.6 %collective-permute-start.8 = (f32[1,1024]{1,0:T(1,128)S(1)}, f32[1,1024]{1,0:T(1,128)S(1)}, u32[]{:S(2)}, u32[]{:S(2)}) collective-permute-start(f32[1,1024]{1,0:T(1,128)S(1)} %multiply_add_fusion.4), channel_id=1, source_target_pairs={{0,96},{16,112},{32,0},{48,16},{64,32},{80,48},{96,64},{112,80},{1... | collective-permute-start | bytes 12296 | tf_op jit(solution)/shard_map/ppermute | solution.py:44
  184.1 4.8 %collective-permute-start.7 = (f32[1,1024]{1,0:T(1,128)S(1)}, f32[1,1024]{1,0:T(1,128)S(1)}, u32[]{:S(2)}, u32[]{:S(2)}) collective-permute-start(f32[1,1024]{1,0:T(1,128)S(1)} %multiply_add_fusion.4), channel_id=1, source_target_pairs={{0,32},{16,48},{32,64},{48,80},{64,96},{80,112},{96,0},{112,16},{1... | collective-permute-start | bytes 12296 | tf_op jit(solution)/shard_map/ppermute | solution.py:44
  190.7 5.2 %collective-permute-start.12 = (f32[1,1024]{1,0:T(1,128)S(1)}, f32[1,1024]{1,0:T(1,128)S(1)}, u32[]{:S(2)}, u32[]{:S(2)}) collective-permute-start(f32[1,1024]{1,0:T(1,128)S(1)} %row_lse.2), channel_id=1, source_target_pairs={{0,2},{1,3},{2,0},{3,1},{4,6},{5,7},{6,4},{7,5},{8,10},{9,11},{10,... | collective-permute-start | bytes 12296 | tf_op jit(solution)/shard_map/ppermute | solution.py:44
  191.1 4.8 %collective-permute-start.11 = (f32[1,1024]{1,0:T(1,128)S(1)}, f32[1,1024]{1,0:T(1,128)S(1)}, u32[]{:S(2)}, u32[]{:S(2)}) collective-permute-start(f32[1,1024]{1,0:T(1,128)S(1)} %row_lse.2), channel_id=1, source_target_pairs={{0,3},{1,0},{2,1},{3,2},{4,7},{5,4},{6,5},{7,6},{8,11},{9,8},{10,9... | collective-permute-start | bytes 12296 | tf_op jit(solution)/shard_map/ppermute | solution.py:44
  192.9 4.8 %collective-permute-start.10 = (f32[1,1024]{1,0:T(1,128)S(1)}, f32[1,1024]{1,0:T(1,128)S(1)}, u32[]{:S(2)}, u32[]{:S(2)}) collective-permute-start(f32[1,1024]{1,0:T(1,128)S(1)} %row_lse.2), channel_id=1, source_target_pairs={{0,1},{1,2},{2,3},{3,0},{4,5},{5,6},{6,7},{7,4},{8,9},{9,10},{10,1... | collective-permute-start | bytes 12296 | tf_op jit(solution)/shard_map/ppermute | solution.py:44
  197.7 5.2 %collective-permute-start.15 = (f32[1,1024]{1,0:T(1,128)S(1)}, f32[1,1024]{1,0:T(1,128)S(1)}, u32[]{:S(2)}, u32[]{:S(2)}) collective-permute-start(f32[1,1024]{1,0:T(1,128)S(1)} %multiply_add_fusion.3), channel_id=1, source_target_pairs={{0,8},{1,9},{2,10},{3,11},{4,12},{5,13},{6,14},{7,15},{8,0},{9,1},... | collective-permute-start | bytes 12296 | tf_op jit(solution)/shard_map/ppermute | solution.py:44
  198.1 4.9 %collective-permute-start.14 = (f32[1,1024]{1,0:T(1,128)S(1)}, f32[1,1024]{1,0:T(1,128)S(1)}, u32[]{:S(2)}, u32[]{:S(2)}) collective-permute-start(f32[1,1024]{1,0:T(1,128)S(1)} %multiply_add_fusion.3), channel_id=1, source_target_pairs={{0,12},{1,13},{2,14},{3,15},{4,0},{5,1},{6,2},{7,3},{8,4},{9,5},{1... | collective-permute-start | bytes 12296 | tf_op jit(solution)/shard_map/ppermute | solution.py:44
  200.1 4.8 %collective-permute-start.13 = (f32[1,1024]{1,0:T(1,128)S(1)}, f32[1,1024]{1,0:T(1,128)S(1)}, u32[]{:S(2)}, u32[]{:S(2)}) collective-permute-start(f32[1,1024]{1,0:T(1,128)S(1)} %multiply_add_fusion.3), channel_id=1, source_target_pairs={{0,4},{1,5},{2,6},{3,7},{4,8},{5,9},{6,10},{7,11},{8,12},{9,13},{1... | collective-permute-start | bytes 12296 | tf_op jit(solution)/shard_map/ppermute | solution.py:44
  206.7 1.2 collective-permute-start.16
  207.9 5.2 %collective-permute-start.19 = (f32[1,1024]{1,0:T(1,128)S(1)}, f32[1,1024]{1,0:T(1,128)S(1)}, u32[]{:S(2)}, u32[]{:S(2)}) collective-permute-start(f32[1,1024]{1,0:T(1,128)S(1)} %multiply_add_fusion.2), channel_id=1, source_target_pairs={{0,64},{16,80},{32,96},{48,112},{64,0},{80,16},{96,32},{112,48},{1... | collective-permute-start | bytes 12296 | tf_op jit(solution)/shard_map/ppermute | solution.py:44
  208.3 4.8 %collective-permute-start.18 = (f32[1,1024]{1,0:T(1,128)S(1)}, f32[1,1024]{1,0:T(1,128)S(1)}, u32[]{:S(2)}, u32[]{:S(2)}) collective-permute-start(f32[1,1024]{1,0:T(1,128)S(1)} %multiply_add_fusion.2), channel_id=1, source_target_pairs={{0,96},{16,112},{32,0},{48,16},{64,32},{80,48},{96,64},{112,80},{1... | collective-permute-start | bytes 12296 | tf_op jit(solution)/shard_map/ppermute | solution.py:44
  210.4 4.8 %collective-permute-start.17 = (f32[1,1024]{1,0:T(1,128)S(1)}, f32[1,1024]{1,0:T(1,128)S(1)}, u32[]{:S(2)}, u32[]{:S(2)}) collective-permute-start(f32[1,1024]{1,0:T(1,128)S(1)} %multiply_add_fusion.2), channel_id=1, source_target_pairs={{0,32},{16,48},{32,64},{48,80},{64,96},{80,112},{96,0},{112,16},{1... | collective-permute-start | bytes 12296 | tf_op jit(solution)/shard_map/ppermute | solution.py:44
  216.9 5.2 %collective-permute-start.22 = (f32[1,1024]{1,0:T(1,128)S(1)}, f32[1,1024]{1,0:T(1,128)S(1)}, u32[]{:S(2)}, u32[]{:S(2)}) collective-permute-start(f32[1,1024]{1,0:T(1,128)S(1)} %row_lse.3), channel_id=1, source_target_pairs={{0,2},{1,3},{2,0},{3,1},{4,6},{5,7},{6,4},{7,5},{8,10},{9,11},{10,... | collective-permute-start | bytes 12296 | tf_op jit(solution)/shard_map/ppermute | solution.py:44
  217.0 5.1 %collective-permute-start.21 = (f32[1,1024]{1,0:T(1,128)S(1)}, f32[1,1024]{1,0:T(1,128)S(1)}, u32[]{:S(2)}, u32[]{:S(2)}) collective-permute-start(f32[1,1024]{1,0:T(1,128)S(1)} %row_lse.3), channel_id=1, source_target_pairs={{0,3},{1,0},{2,1},{3,2},{4,7},{5,4},{6,5},{7,6},{8,11},{9,8},{10,9... | collective-permute-start | bytes 12296 | tf_op jit(solution)/shard_map/ppermute | solution.py:44
  218.5 4.8 %collective-permute-start.20 = (f32[1,1024]{1,0:T(1,128)S(1)}, f32[1,1024]{1,0:T(1,128)S(1)}, u32[]{:S(2)}, u32[]{:S(2)}) collective-permute-start(f32[1,1024]{1,0:T(1,128)S(1)} %row_lse.3), channel_id=1, source_target_pairs={{0,1},{1,2},{2,3},{3,0},{4,5},{5,6},{6,7},{7,4},{8,9},{9,10},{10,1... | collective-permute-start | bytes 12296 | tf_op jit(solution)/shard_map/ppermute | solution.py:44
  223.3 5.2 %collective-permute-start.25 = (f32[1,1024]{1,0:T(1,128)S(1)}, f32[1,1024]{1,0:T(1,128)S(1)}, u32[]{:S(2)}, u32[]{:S(2)}) collective-permute-start(f32[1,1024]{1,0:T(1,128)S(1)} %multiply_add_fusion.1), channel_id=1, source_target_pairs={{0,8},{1,9},{2,10},{3,11},{4,12},{5,13},{6,14},{7,15},{8,0},{9,1},... | collective-permute-start | bytes 12296 | tf_op jit(solution)/shard_map/ppermute | solution.py:44
  223.7 4.8 %collective-permute-start.24 = (f32[1,1024]{1,0:T(1,128)S(1)}, f32[1,1024]{1,0:T(1,128)S(1)}, u32[]{:S(2)}, u32[]{:S(2)}) collective-permute-start(f32[1,1024]{1,0:T(1,128)S(1)} %multiply_add_fusion.1), channel_id=1, source_target_pairs={{0,12},{1,13},{2,14},{3,15},{4,0},{5,1},{6,2},{7,3},{8,4},{9,5},{1... | collective-permute-start | bytes 12296 | tf_op jit(solution)/shard_map/ppermute | solution.py:44
  224.9 4.8 %collective-permute-start.23 = (f32[1,1024]{1,0:T(1,128)S(1)}, f32[1,1024]{1,0:T(1,128)S(1)}, u32[]{:S(2)}, u32[]{:S(2)}) collective-permute-start(f32[1,1024]{1,0:T(1,128)S(1)} %multiply_add_fusion.1), channel_id=1, source_target_pairs={{0,4},{1,5},{2,6},{3,7},{4,8},{5,9},{6,10},{7,11},{8,12},{9,13},{1... | collective-permute-start | bytes 12296 | tf_op jit(solution)/shard_map/ppermute | solution.py:44
  232.1 1.2 collective-permute-start.26
  233.4 5.2 %collective-permute-start.29 = (f32[1,1024]{1,0:T(1,128)S(1)}, f32[1,1024]{1,0:T(1,128)S(1)}, u32[]{:S(2)}, u32[]{:S(2)}) collective-permute-start(f32[1,1024]{1,0:T(1,128)S(1)} %multiply_add_fusion), channel_id=1, source_target_pairs={{0,64},{16,80},{32,96},{48,112},{64,0},{80,16},{96,32},{112,48},{1... | collective-permute-start | bytes 12296 | tf_op jit(solution)/shard_map/ppermute | solution.py:44
  233.5 5.1 %collective-permute-start.28 = (f32[1,1024]{1,0:T(1,128)S(1)}, f32[1,1024]{1,0:T(1,128)S(1)}, u32[]{:S(2)}, u32[]{:S(2)}) collective-permute-start(f32[1,1024]{1,0:T(1,128)S(1)} %multiply_add_fusion), channel_id=1, source_target_pairs={{0,96},{16,112},{32,0},{48,16},{64,32},{80,48},{96,64},{112,80},{1... | collective-permute-start | bytes 12296 | tf_op jit(solution)/shard_map/ppermute | solution.py:44
  234.9 4.8 %collective-permute-start.27 = (f32[1,1024]{1,0:T(1,128)S(1)}, f32[1,1024]{1,0:T(1,128)S(1)}, u32[]{:S(2)}, u32[]{:S(2)}) collective-permute-start(f32[1,1024]{1,0:T(1,128)S(1)} %multiply_add_fusion), channel_id=1, source_target_pairs={{0,32},{16,48},{32,64},{48,80},{64,96},{80,112},{96,0},{112,16},{1... | collective-permute-start | bytes 12296 | tf_op jit(solution)/shard_map/ppermute | solution.py:44
  255.6 5.2 %collective-permute-start.32 = (f32[1,1024]{1,0:T(1,128)S(1)}, f32[1,1024]{1,0:T(1,128)S(1)}, u32[]{:S(2)}, u32[]{:S(2)}) collective-permute-start(f32[1,1024]{1,0:T(1,128)S(1)} %get-tuple-element.10), channel_id=1, source_target_pairs={{0,2},{1,3},{2,0},{3,1},{4,6},{5,7},{6,4},{7,5},{8,10},{9,11},{10,... | collective-permute-start | bytes 12296 | tf_op jit(solution)/shard_map/ppermute | solution.py:44
  256.6 4.1 %collective-permute-start.31 = (f32[1,1024]{1,0:T(1,128)S(1)}, f32[1,1024]{1,0:T(1,128)S(1)}, u32[]{:S(2)}, u32[]{:S(2)}) collective-permute-start(f32[1,1024]{1,0:T(1,128)S(1)} %get-tuple-element.10), channel_id=1, source_target_pairs={{0,3},{1,0},{2,1},{3,2},{4,7},{5,4},{6,5},{7,6},{8,11},{9,8},{10,9... | collective-permute-start | bytes 12296 | tf_op jit(solution)/shard_map/ppermute | solution.py:44
  257.8 4.8 %collective-permute-start.30 = (f32[1,1024]{1,0:T(1,128)S(1)}, f32[1,1024]{1,0:T(1,128)S(1)}, u32[]{:S(2)}, u32[]{:S(2)}) collective-permute-start(f32[1,1024]{1,0:T(1,128)S(1)} %get-tuple-element.10), channel_id=1, source_target_pairs={{0,1},{1,2},{2,3},{3,0},{4,5},{5,6},{6,7},{7,4},{8,9},{9,10},{10,1... | collective-permute-start | bytes 12296 | tf_op jit(solution)/shard_map/ppermute | solution.py:44
  262.7 5.2 %collective-permute-start.35 = (f32[1,1024]{1,0:T(1,128)S(1)}, f32[1,1024]{1,0:T(1,128)S(1)}, u32[]{:S(2)}, u32[]{:S(2)}) collective-permute-start(f32[1,1024]{1,0:T(1,128)S(1)} %add_add_fusion.1), channel_id=1, source_target_pairs={{0,8},{1,9},{2,10},{3,11},{4,12},{5,13},{6,14},{7,15},{8,0},{9,1},... | collective-permute-start | bytes 12296 | tf_op jit(solution)/shard_map/ppermute | solution.py:44
  263.6 4.2 %collective-permute-start.34 = (f32[1,1024]{1,0:T(1,128)S(1)}, f32[1,1024]{1,0:T(1,128)S(1)}, u32[]{:S(2)}, u32[]{:S(2)}) collective-permute-start(f32[1,1024]{1,0:T(1,128)S(1)} %add_add_fusion.1), channel_id=1, source_target_pairs={{0,12},{1,13},{2,14},{3,15},{4,0},{5,1},{6,2},{7,3},{8,4},{9,5},{1... | collective-permute-start | bytes 12296 | tf_op jit(solution)/shard_map/ppermute | solution.py:44
  264.8 4.8 %collective-permute-start.33 = (f32[1,1024]{1,0:T(1,128)S(1)}, f32[1,1024]{1,0:T(1,128)S(1)}, u32[]{:S(2)}, u32[]{:S(2)}) collective-permute-start(f32[1,1024]{1,0:T(1,128)S(1)} %add_add_fusion.1), channel_id=1, source_target_pairs={{0,4},{1,5},{2,6},{3,7},{4,8},{5,9},{6,10},{7,11},{8,12},{9,13},{1... | collective-permute-start | bytes 12296 | tf_op jit(solution)/shard_map/ppermute | solution.py:44
Sparse Core Ops, SparseCore 0:
  9.7 52.1 all-gather.4
  64.0 78.6 all-gather.2
  255.7 80.9 reduce-scatter.1

commit v2 on v1

--- a/solution.py
+++ b/solution.py
@@ -52,6 +52,115 @@
 def over_row(value, combine):
     value = over(value, "row", [swap_core()], combine)
     return over(value, "row", [shift_y(b) for b in (1, 3, 2)], combine)
+
+
+BOTH = ("row", "col")
+
+
+def shift_noise(by, first):
+    pairs = []
+    for y in range(NY):
+        for c in range(NC):
+            for x in range(NX):
+                for z in range(NZ):
+                    to_x, to_z = (x, (z + by) % NZ) if (c == 0) == first else ((x + by) % NX, z)
+                    base = (y * NC + c) * NX * NZ
+                    pairs.append((base + x * NZ + z, base + to_x * NZ + to_z))
+    return pairs
+
+
+def spread_y():
+    return [
+        (y * NC + c, (y + 1 - 2 * c) % NY * NC + c) for y in range(NY) for c in range(NC)
+    ]
+
+
+ORDER = (0, 3, 1, 2)
+
+
+def hop_f(value, by):
+    return lax.ppermute(value, BOTH, shift_noise(by, True))
+
+
+def hop_s(value, by):
+    return lax.ppermute(value, BOTH, shift_noise(by, False))
+
+
+def block_at(df, ds):
+    core = lax.axis_index("row") % NC
+    col = lax.axis_index("col")
+    dz = jnp.where(core == 0, df, ds)
+    dx = jnp.where(core == 0, ds, df)
+    return (col // NZ + dx) % NX * NZ + (col % NZ + dz) % NZ
+
+
+def gather_noise(noise):
+    rows = noise.shape[0]
+    half = rows // 2
+    line = [noise, hop_f(noise, 1), hop_f(noise, -1), hop_f(noise, 2)]
+    top = jnp.concatenate([v[:half] for v in line], axis=0)
+    end = jnp.concatenate([v[half:] for v in line], axis=0)
+    top_m, end_p = hop_s(top, 1), hop_s(end, -1)
+    end_m, top_p = hop_s(end, 1), hop_s(top, -1)
+    top_far, end_far = hop_s(top_m, 1), hop_s(end_p, -1)
+    pieces, plan, at = [], [], []
+    for v, df in zip(line, ORDER):
+        plan.append((len(pieces), 0, rows, 0, len(at)))
+        at.append(block_at(df, 0))
+        pieces.append(v)
+    for v, row, ds in (
+        (top_m, 0, 3), (end_m, half, 3), (top_p, 0, 1), (end_p, half, 1),
+        (top_far, 0, 2), (end_far, half, 2),
+    ):
+        for k, df in enumerate(ORDER):
+            plan.append((len(pieces), k * half, half, row, len(at)))
+            at.append(block_at(df, ds))
+        pieces.append(v)
+    return pieces, plan, at
+
+
+def gather_latents(latents):
+    cols = latents.shape[0]
+    swap = lambda v: lax.ppermute(v, "row", swap_core())
+    onward = lambda v: lax.ppermute(v, "row", spread_y())
+    near = onward(latents)
+    other = swap(latents)
+    near_2 = onward(other)
+    far = onward(near)
+    pieces = [latents, other, near, near_2, far, swap(near), swap(near_2), swap(far)]
+    row = lax.axis_index("row")
+    y, core = row // NC, row % NC
+    block = lambda dy, flip: (y + dy) % NY * NC + (core if not flip else 1 - core)
+    back = jnp.where(core == 0, 3, 1)
+    plan = [(k, 0, cols, 0, k) for k in range(8)]
+    at = [
+        block(0, False), block(0, True),
+        block(back, False), block(back, True), block(2, False),
+        block(4 - back, True), block(4 - back, False), block(2, True),
+    ]
+    return pieces, plan, at
+
+
+def scatter_sum(plan, lat, far_top, far_end):
+    blocks = lambda ds: jnp.stack([block_at(df, ds) for df in ORDER]).astype(jnp.int32)
+    after, before = blocks(1), blocks(3)
+    far_top, far_end = hop_s(far_top, 1), hop_s(far_end, -1)
+    end_m = hop_s(share_call(plan, lat, after, 1), 1)
+    top_p = hop_s(share_call(plan, lat, before, 0), -1)
+    own = share_call(plan, lat, blocks(0), None)
+    top_m = hop_s(share_call(plan, lat, after, 0, far_top), 1)
+    end_p = hop_s(share_call(plan, lat, before, 1, far_end), -1)
+    half, width = top_m.shape[0], top_m.shape[1] // 4
+    sums = []
+    for k in range(4):
+        lanes = slice(k * width, (k + 1) * width)
+        top = own[:half, lanes] + top_m[:, lanes].astype(F32) + top_p[:, lanes].astype(F32)
+        end = own[half:, lanes] + end_m[:, lanes].astype(F32) + end_p[:, lanes].astype(F32)
+        sums.append(jnp.concatenate([top, end], axis=0))
+    total = sums[0]
+    for value, df in zip(sums[1:], ORDER[1:]):
+        total = total + hop_f(value.astype(BF16), df).astype(F32)
+    return total
 
 
 def eye():
@@ -93,36 +202,100 @@
     out[...] = to_lanes(jnp.concatenate(columns, axis=0))
 
 
-def cross_kernel(scale, noise_ref, lat_ref, logits_ref, lse_ref):
-    cross = lax.dot_general(
-        noise_ref[...], lat_ref[...], (((1,), (1,)), ((), ())), preferred_element_type=F32
-    )
-    logits_ref[...] = cross * scale
-    row_lse_block(lambda at, n: logits_ref[pl.ds(at, n), :], noise_ref.shape[0], lse_ref)
-
-
-def cross_call(noise, lat, scale):
-    rows, width = noise.shape
-    cols = lat.shape[0]
+def cross_kernel(scale, noise_plan, lat_plan, at_ref, *refs):
+    counts = (1 + max(p[0] for p in noise_plan), 1 + max(p[0] for p in lat_plan))
+    noise_refs, lat_refs = refs[: counts[0]], refs[counts[0] : sum(counts)]
+    logits_ref, lse_ref, lat_out, noise_buf, lat_buf, noise_sem, lat_sem, out_sem = refs[sum(counts) :]
+    rows, width = noise_buf.shape
+    part = width // 4
+    quarters = [lax.rem(at_ref[at_ref.shape[0] - 1] + k, 4) for k in (0, 3, 1, 2)]
+    for quarter in quarters:
+        for plan, sources, buf, sem in (
+            (lat_plan, lat_refs, lat_buf, lat_sem),
+            (noise_plan, noise_refs, noise_buf, noise_sem),
+        ):
+            for piece, first, count, row, entry in plan:
+                wide = sources[piece].shape[1]
+                lane = at_ref[entry] * wide
+
+                @pl.when(lax.div(lane, part) == quarter)
+                def start():
+                    pltpu.make_async_copy(
+                        sources[piece].at[pl.ds(first, count), :],
+                        buf.at[pl.ds(row, count), pl.ds(pl.multiple_of(lane, wide), wide)],
+                        sem.at[quarter],
+                    ).start()
+
     block = 256
+    outs = []
+    for j, quarter in enumerate(quarters):
+        lanes = pl.ds(pl.multiple_of(quarter * part, part), part)
+        for buf, sem in ((lat_buf, lat_sem), (noise_buf, noise_sem)):
+            pltpu.make_async_copy(buf.at[:, lanes], buf.at[:, lanes], sem.at[quarter]).wait()
+        outs.append(pltpu.make_async_copy(lat_buf.at[:, lanes], lat_out.at[:, lanes], out_sem.at[j]))
+        outs[-1].start()
+
+        def some_rows(i, _):
+            at = pl.ds(pl.multiple_of(i * block, block), block)
+            cross = lax.dot_general(
+                noise_buf[at, lanes],
+                lat_buf[:, lanes],
+                (((1,), (1,)), ((), ())),
+                preferred_element_type=F32,
+            )
+            if j:
+                cross = logits_ref[at, :] + cross
+            if j == 3:
+                cross = cross * scale
+            logits_ref[at, :] = cross
+            if j == 3:
+                row_lse_block(
+                    lambda k, n: logits_ref[pl.ds(pl.multiple_of(i * block, block) + k, n), :],
+                    block,
+                    lse_ref.at[:, at],
+                )
+            return 0
+
+        lax.fori_loop(0, rows // block, some_rows, 0)
+    for out in outs:
+        out.wait()
+
+
+def cross_call(noise, lat, cols, width, scale):
+    pieces = noise[0] + lat[0]
+    rows = noise[0][0].shape[0]
+    shift = len(noise[2])
+    lat_plan = [(p, f, c, r, e + shift) for p, f, c, r, e in lat[1]]
+    first = lax.axis_index("col") // NZ
     return pl.pallas_call(
-        functools.partial(cross_kernel, scale),
-        grid=(rows // block,),
-        in_specs=[
-            pl.BlockSpec((block, width), lambda i: (i, 0)),
-            pl.BlockSpec((cols, width), lambda i: (0, 0)),
-        ],
+        functools.partial(cross_kernel, scale, noise[1], lat_plan),
+        in_specs=[pl.BlockSpec(memory_space=pltpu.SMEM)]
+        + [pl.BlockSpec(memory_space=pltpu.HBM)] * len(pieces),
         out_specs=[
-            pl.BlockSpec((block, cols), lambda i: (i, 0)),
-            pl.BlockSpec((1, block), lambda i: (0, i)),
+            pl.BlockSpec(memory_space=pltpu.VMEM),
+            pl.BlockSpec(memory_space=pltpu.VMEM),
+            pl.BlockSpec(memory_space=pltpu.HBM),
         ],
         out_shape=[
             jax.ShapeDtypeStruct((rows, cols), F32),
             jax.ShapeDtypeStruct((1, rows), F32),
-        ],
-        compiler_params=pltpu.CompilerParams(vmem_limit_bytes=40 * 2**20),
+            jax.ShapeDtypeStruct((cols, width), BF16),
+        ],
+        scratch_shapes=[
+            pltpu.VMEM((rows, width), BF16),
+            pltpu.VMEM((cols, width), BF16),
+            pltpu.SemaphoreType.DMA((4,)),
+            pltpu.SemaphoreType.DMA((4,)),
+            pltpu.SemaphoreType.DMA((4,)),
+        ],
+        cost_estimate=pl.CostEstimate(
+            flops=2 * rows * cols * width,
+            bytes_accessed=2 * (rows + 2 * cols) * width + 4 * rows * cols,
+            transcendentals=rows * cols,
+        ),
+        compiler_params=pltpu.CompilerParams(vmem_limit_bytes=32 * 2**20),
         name="cross",
-    )(noise, lat)
+    )(jnp.stack(noise[2] + lat[2] + [first]).astype(jnp.int32), *pieces)
 
 
 def row_kernel(logits_ref, colpot_ref, lse_ref):
@@ -187,54 +360,119 @@
     )(logits, rowpot)
 
 
-def plan_kernel(logits_ref, rowpot_ref, colpot_ref, lat_ref, share_ref, mass_ref):
-    rowpot = to_sublanes(rowpot_ref[...])
-    plan = jnp.exp2(logits_ref[...] + rowpot + colpot_ref[...]).astype(BF16)
-    mass_ref[...] = to_lanes(jnp.sum(plan.astype(F32), axis=1, keepdims=True))
-    share_ref[...] = jnp.dot(plan, lat_ref[...], preferred_element_type=F32).astype(BF16)
-
-
-def plan_call(logits, rowpot, colpot, lat):
+def plan_kernel(blocks_ref, logits_ref, rowpot_ref, colpot_ref, lat_ref, plan_ref, mass_ref, top_ref, end_ref):
+    rows = logits_ref.shape[0]
+    half = rows // 2
+
+    @pl.when(pl.program_id(0) == 0)
+    def make_plan():
+        colpot = colpot_ref[...]
+        step = 128
+        for at in range(0, rows, step):
+            rowpot = to_sublanes(rowpot_ref[:, pl.ds(at, step)])
+            plan = jnp.exp2(logits_ref[pl.ds(at, step), :] + rowpot + colpot).astype(BF16)
+            plan_ref[pl.ds(at, step), :] = plan
+            mass = jnp.sum(plan.astype(F32), axis=1, keepdims=True)
+            mass_ref[:, pl.ds(at, step)] = to_lanes(mass)
+
+    lat = lat_ref[...]
+    top_ref[...] = jnp.dot(plan_ref[:half, :], lat, preferred_element_type=F32).astype(BF16)
+    end_ref[...] = jnp.dot(plan_ref[half:, :], lat, preferred_element_type=F32).astype(BF16)
+
+
+def plan_call(logits, rowpot, colpot, lat, blocks):
     rows, cols = logits.shape
-    width = lat.shape[1]
-    block = 256
+    width = lat.shape[1] // (NX * NZ)
+    whole = lambda i, b: (0, 0)
     return pl.pallas_call(
         plan_kernel,
-        grid=(rows // block,),
-        in_specs=[
-            pl.BlockSpec((block, cols), lambda i: (i, 0)),
-            pl.BlockSpec((1, block), lambda i: (0, i)),
-            pl.BlockSpec((1, cols), lambda i: (0, 0)),
-            pl.BlockSpec((cols, width), lambda i: (0, 0)),
-        ],
-        out_specs=[
-            pl.BlockSpec((block, width), lambda i: (i, 0)),
-            pl.BlockSpec((1, block), lambda i: (0, i)),
-        ],
+        grid_spec=pltpu.PrefetchScalarGridSpec(
+            num_scalar_prefetch=1,
+            grid=(4,),
+            in_specs=[
+                pl.BlockSpec((rows, cols), whole),
+                pl.BlockSpec((1, rows), whole),
+                pl.BlockSpec((1, cols), whole),
+                pl.BlockSpec((cols, width), lambda i, b: (0, b[i])),
+            ],
+            out_specs=[
+                pl.BlockSpec((rows, cols), whole),
+                pl.BlockSpec((1, rows), whole),
+                pl.BlockSpec((rows // 2, width), lambda i, b: (0, i)),
+                pl.BlockSpec((rows // 2, width), lambda i, b: (0, i)),
+            ],
+        ),
         out_shape=[
-            jax.ShapeDtypeStruct((rows, width), BF16),
+            jax.ShapeDtypeStruct((rows, cols), BF16),
             jax.ShapeDtypeStruct((1, rows), F32),
-        ],
-        compiler_params=pltpu.CompilerParams(vmem_limit_bytes=48 * 2**20),
+            jax.ShapeDtypeStruct((rows // 2, 4 * width), BF16),
+            jax.ShapeDtypeStruct((rows // 2, 4 * width), BF16),
+        ],
+        cost_estimate=pl.CostEstimate(
+            flops=2 * rows * cols * 4 * width,
+            bytes_accessed=2 * (rows + cols) * 4 * width + 6 * rows * cols,
+            transcendentals=rows * cols,
+        ),
+        compiler_params=pltpu.CompilerParams(vmem_limit_bytes=32 * 2**20),
         name="plan",
-    )(logits, rowpot, colpot, lat)
+    )(blocks, logits, rowpot, colpot, lat)
+
+
+def share_kernel(blocks_ref, plan_ref, lat_ref, *refs):
+    share = jnp.dot(plan_ref[...], lat_ref[...], preferred_element_type=F32)
+    if len(refs) == 2:
+        share = share + refs[0][...].astype(F32)
+    refs[-1][...] = share.astype(refs[-1].dtype)
+
+
+def share_call(plan, lat, blocks, part, more=None):
+    rows, cols = plan.shape
+    width = lat.shape[1] // (NX * NZ)
+    count, first = (rows, 0) if part is None else (rows // 2, part)
+    spot = pl.BlockSpec((count, width), lambda i, b: (0, i))
+    return pl.pallas_call(
+        share_kernel,
+        grid_spec=pltpu.PrefetchScalarGridSpec(
+            num_scalar_prefetch=1,
+            grid=(4,),
+            in_specs=[
+                pl.BlockSpec((count, cols), lambda i, b: (first, 0)),
+                pl.BlockSpec((cols, width), lambda i, b: (0, b[i])),
+            ]
+            + ([] if more is None else [spot]),
+            out_specs=spot,
+        ),
+        out_shape=jax.ShapeDtypeStruct((count, 4 * width), F32 if part is None else BF16),
+        cost_estimate=pl.CostEstimate(
+            flops=2 * count * cols * 4 * width,
+            bytes_accessed=2 * (count * cols + cols * 4 * width + 2 * count * 4 * width),
+            transcendentals=0,
+        ),
+        compiler_params=pltpu.CompilerParams(vmem_limit_bytes=24 * 2**20),
+        name="share",
+    )(blocks, plan, lat, *([] if more is None else [more]))
 
 
 def on_device(noise, latents):
-    whole_lat = lax.all_gather(latents, "row", axis=1, tiled=True)
-    whole_noise = lax.all_gather(noise, "col", axis=1, tiled=True)
-    width = whole_lat.shape[1]
+    width = latents.shape[1] * lax.axis_size("row")
     noise_count = noise.shape[0] * lax.axis_size("row")
     latent_count = latents.shape[0] * lax.axis_size("col")
-    logits, lse = cross_call(whole_noise, whole_lat, 2.0 / (width * EPSILON) * LOG2E)
+    logits, lse, whole_lat = cross_call(
+        gather_noise(noise),
+        gather_latents(latents),
+        latents.shape[0],
+        width,
+        2.0 / (width * EPSILON) * LOG2E,
+    )
     for step in range(ITERS):
         if step:
             lse = row_call(logits, colpot)
         rowpot = -math.log2(noise_count) - over_col(lse, logadd)
         colpot = -math.log2(latent_count) - over_row(col_call(logits, rowpot), logadd)
-    share, mass = plan_call(logits, rowpot, colpot, whole_lat)
+    far = jnp.stack([block_at(df, 2) for df in ORDER]).astype(jnp.int32)
+    plan, mass, far_top, far_end = plan_call(logits, rowpot, colpot, whole_lat, far)
+    total = scatter_sum(plan, whole_lat, far_top, far_end)
     mass = over_col(mass, lambda parts: functools.reduce(jnp.add, parts))
-    total = lax.psum_scatter(share, "col", scatter_dimension=1, tiled=True).astype(F32)
     transported = (total / mass.reshape(-1, 1)).astype(BF16)
     return (transported, rowpot.reshape(-1) * LN2, colpot.reshape(-1) * LN2)
 

time: 346 us -> 249 us (0.72)
  waiting for transfers between devices: 254 us -> 127 us
  starting transfers between devices: 32.9 us -> 63.8 us
  between operations: 13.9 us -> 1.04 us
  Pallas kernels: 37.8 us -> 44.7 us
  local copies, waits for them, and re-layouts: 3.38 us -> 7.94 us
    all_gather x2 -> x0, waiting for transfers between devices: 134 us -> none  [the longest x1 80.8 us: on_device(): whole_noise = lax.all_gather(noise, 'col', axis=1, tiled=True)]
    reduce_scatter x1 -> x0, waiting for transfers between devices: 67 us -> none  [on_device(): lax.psum_scatter(share, 'col', scatter_dimension=1, tiled=True).astype(F32)]
    ppermute x0 -> x25, waiting for transfers between devices: none -> 64.9 us  [the longest x12 53.1 us: hop_s(): return lax.ppermute(value, BOTH, shift_noise(by, False))]
    ppermute x0 -> x25, starting transfers between devices: none -> 28.1 us  [the longest x12 14.6 us: hop_s(): return lax.ppermute(value, BOTH, shift_noise(by, False))]
    ppermute x36, waiting for transfers between devices: 51.1 us -> 62.4 us  [over(): return combine([value] + [lax.ppermute(value, axis, p) for p in perms])]
    pallas_call x2 -> x7, Pallas kernels: 29.4 us -> 36.4 us  [the longest x1 15.9 us: cross_call(): pl.pallas_call(functools.partial(cross_kernel, scale, noise[1], lat_plan)...]
  transfers between devices with their start and end apart: 39 -> 61, of which waited for: 29 -> 39; matrix products, arithmetic and copies ran while one was open for 0% -> 1% of each run, Pallas kernels for 0% -> 6%
where the time goes in v2:
time: 249 us
  waiting for transfers between devices  127 us (51%)
  starting transfers between devices  63.8 us (26%)
  Pallas kernels  44.7 us (18%)
  local copies, waits for them, and re-layouts  7.94 us (3%)
  other arithmetic  4.06 us (2%)
    ppermute x36, waiting for transfers between devices, over(): return combine([value] + [lax.ppermute(value, axis, p) for p in perms])  62.4 us
    ppermute x12, waiting for transfers between devices, hop_s(): return lax.ppermute(value, BOTH, shift_noise(by, False))  53.1 us
    ppermute x36, starting transfers between devices, over(): return combine([value] + [lax.ppermute(value, axis, p) for p in perms])  35.7 us
    pallas_call x1, Pallas kernels, cross_call(): pl.pallas_call(functools.partial(cross_kernel, scale, noise[1], lat_plan)...  15.9 us
    pallas_call x5, Pallas kernels, share_call(): pl.pallas_call(share_kernel, grid_spec=pltpu.PrefetchScalarGridSpec(num_s...  15.4 us
    ppermute x12, starting transfers between devices, hop_s(): return lax.ppermute(value, BOTH, shift_noise(by, False))  14.6 us
    ppermute x6, waiting for transfers between devices, hop_f(): return lax.ppermute(value, BOTH, shift_noise(by, True))  9.34 us
    ppermute x6, starting transfers between devices, hop_f(): return lax.ppermute(value, BOTH, shift_noise(by, True))  8.72 us
  transfers between devices with their start and end apart: 61, of which 39 were waited for; matrix products, arithmetic and copies ran while one was open for 1% of the time, Pallas kernels for 6%

profile of v2, /device:TPU:0, one launch (start us, length us, event | category | flops | bytes accessed | tf_op | source)
XLA Modules:
  0.0 248.8 jit_solution(16317112276520276373)
XLA Ops:
  0.6 4.0 %collective-permute-start.2 = (bf16[1024,256]{1,0:T(8,128)(2,1)}, bf16[1024,256]{1,0:T(8,128)(2,1)S(1)}, u32[]{:S(2)}, u32[]{:S(2)}) collective-permute-start(bf16[1024,256]{1,0:T(8,128)(2,1)} %refs_0_.1), channel_id=1, source_target_pairs={{0,2},{1,3},{2,0},{3,1},{4,6},{5,7},{6,4},{7,5},{8,10},{9,11},{10,... | collective-permute-start | bytes 1572872 | tf_op jit(solution)/shard_map/ppermute | solution.py:82
  6.7 1.6 collective-permute-start.10
  9.3 2.8 %collective-permute-done.2.refs_3_ = bf16[1024,256]{1,0:T(8,128)(2,1)S(1)} collective-permute-done((bf16[1024,256]{1,0:T(8,128)(2,1)}, bf16[1024,256]{1,0:T(8,128)(2,1)S(1)}, u32[]{:S(2)}, u32[]{:S(2)}) %collective-permute-start.2) | collective-permute-done | bytes 524320 | tf_op jit(solution)/shard_map/ppermute | solution.py:82
  12.2 6.5 %collective-permute-done.1.refs_2_ = bf16[1024,256]{1,0:T(8,128)(2,1)S(1)} collective-permute-done((bf16[1024,256]{1,0:T(8,128)(2,1)}, bf16[1024,256]{1,0:T(8,128)(2,1)S(1)}, u32[]{:S(2)}, u32[]{:S(2)}) %collective-permute-start.1) | collective-permute-done | bytes 524320 | tf_op jit(solution)/shard_map/ppermute | solution.py:82
  18.9 2.8 %collective-permute-start.5 = (bf16[2048,256]{1,0:T(8,128)(2,1)S(1)}, bf16[2048,256]{1,0:T(8,128)(2,1)S(1)}, u32[]{:S(2)}, u32[]{:S(2)}) collective-permute-start(bf16[2048,256]{1,0:T(8,128)(2,1)S(1)} %pad_maximum_fusion), channel_id=1, source_target_pairs={{0,12},{1,13},{2,14},{3,15},{4,0},{5,1},{6,2},{7,3},{8,4},{9,5},{1... | collective-permute-start | bytes 3145736 | tf_op jit(solution)/shard_map/ppermute | solution.py:86
  21.8 3.3 %collective-permute-start.6 = (bf16[2048,256]{1,0:T(8,128)(2,1)S(1)}, bf16[2048,256]{1,0:T(8,128)(2,1)}, u32[]{:S(2)}, u32[]{:S(2)}) collective-permute-start(bf16[2048,256]{1,0:T(8,128)(2,1)S(1)} %pad_maximum_fusion.1), channel_id=1, source_target_pairs={{0,12},{1,13},{2,14},{3,15},{4,0},{5,1},{6,2},{7,3},{8,4},{9,5},{1... | collective-permute-start | bytes 3145736 | tf_op jit(solution)/shard_map/ppermute | solution.py:86
  25.1 1.6 collective-permute-start.11
  27.7 6.3 %collective-permute-done.5.refs_6_ = bf16[2048,256]{1,0:T(8,128)(2,1)S(1)} collective-permute-done((bf16[2048,256]{1,0:T(8,128)(2,1)S(1)}, bf16[2048,256]{1,0:T(8,128)(2,1)S(1)}, u32[]{:S(2)}, u32[]{:S(2)}) %collective-permute-start.5) | collective-permute-done | bytes 1048608 | tf_op jit(solution)/shard_map/ppermute | solution.py:86
  35.1 1.6 collective-permute-start.12
  37.9 7.4 %collective-permute-done.6.refs_7_ = bf16[2048,256]{1,0:T(8,128)(2,1)} collective-permute-done((bf16[2048,256]{1,0:T(8,128)(2,1)S(1)}, bf16[2048,256]{1,0:T(8,128)(2,1)}, u32[]{:S(2)}, u32[]{:S(2)}) %collective-permute-start.6) | collective-permute-done | bytes 1048608 | tf_op jit(solution)/shard_map/ppermute | solution.py:86
  45.3 1.3 collective-permute-start.7
  46.6 2.4 collective-permute-done.4.refs_5_
  50.1 2.4 collective-permute-done.12.refs_14_
  52.7 9.5 %collective-permute-done.7.refs_8_ = bf16[2048,256]{1,0:T(8,128)(2,1)} collective-permute-done((bf16[2048,256]{1,0:T(8,128)(2,1)}, bf16[2048,256]{1,0:T(8,128)(2,1)}, u32[]{:S(2)}, u32[]{:S(2)}) %collective-permute-start.7) | collective-permute-done | bytes 1048608 | tf_op jit(solution)/shard_map/ppermute | solution.py:86
  62.2 2.9 %collective-permute-done.8.refs_9_ = bf16[2048,256]{1,0:T(8,128)(2,1)} collective-permute-done((bf16[2048,256]{1,0:T(8,128)(2,1)}, bf16[2048,256]{1,0:T(8,128)(2,1)}, u32[]{:S(2)}, u32[]{:S(2)}) %collective-permute-start.8) | collective-permute-done | bytes 1048608 | tf_op jit(solution)/shard_map/ppermute | solution.py:86
  68.8 15.9 %cross.1 = (f32[1024,1024]{1,0:T(8,128)S(1)}, f32[1,1024]{1,0:T(1,128)S(1)}, bf16[1024,4096]{1,0:T(8,128)(2,1)}) custom-call(s32[37]{0:T(128)S(1)} %stack.145.at_ref, bf16[1024,256]{1,0:T(8,128)(2,1)S(1)} %copy-done, bf16[1024,256]{1,0:T(8,128)(2,1)S(1)} %collective-permute-done.refs_1_, bf16[1024,256]{1,0:T(8,128)(2,1)S(1)} %collective-permute-done.1.refs_2_, ...), custom_call_target="tpu_custom_call" | custom-call | flops 8589934592 | bytes 29360128 | tf_op jit(solution)/shard_map/cross/pallas_call | solution.py:270
  84.7 2.7 %collective-permute-start.18 = (f32[1,1024]{1,0:T(1,128)S(1)}, f32[1,1024]{1,0:T(1,128)S(1)}, u32[]{:S(2)}, u32[]{:S(2)}) collective-permute-start(f32[1,1024]{1,0:T(1,128)S(1)} %get-tuple-element.11), channel_id=1, source_target_pairs={{0,2},{1,3},{2,0},{3,1},{4,6},{5,7},{6,4},{7,5},{8,10},{9,11},{10,... | collective-permute-start | bytes 12296 | tf_op jit(solution)/shard_map/ppermute | solution.py:44
  90.9 2.4 collective-permute-done.16
  93.4 1.6 collective-permute-start.21
  95.7 1.4 collective-permute-start.19
  97.1 1.5 collective-permute-done.21
  98.7 1.8 collective-permute-done.19
  100.6 1.7 col_lse.3
  103.5 3.3 %collective-permute-start.25 = (f32[1,1024]{1,0:T(1,128)S(1)}, f32[1,1024]{1,0:T(1,128)S(1)}, u32[]{:S(2)}, u32[]{:S(2)}) collective-permute-start(f32[1,1024]{1,0:T(1,128)S(1)} %multiply_add_fusion.4), channel_id=1, source_target_pairs={{0,64},{16,80},{32,96},{48,112},{64,0},{80,16},{96,32},{112,48},{1... | collective-permute-start | bytes 12296 | tf_op jit(solution)/shard_map/ppermute | solution.py:44
  108.8 1.6 collective-permute-done.24
  110.4 2.3 collective-permute-done.23
  112.7 1.7 row_lse.2
  115.2 1.6 collective-permute-start.27
  117.2 2.4 collective-permute-done.28
  119.6 2.0 collective-permute-done.26
  122.5 2.0 collective-permute-start.30
  124.6 2.3 collective-permute-done.31
  126.8 2.6 %collective-permute-done.29 = f32[1,1024]{1,0:T(1,128)S(1)} collective-permute-done((f32[1,1024]{1,0:T(1,128)S(1)}, f32[1,1024]{1,0:T(1,128)S(1)}, u32[]{:S(2)}, u32[]{:S(2)}) %collective-permute-start.29) | collective-permute-done | bytes 4128 | tf_op jit(solution)/shard_map/ppermute | solution.py:44
  129.4 1.7 col_lse.4
  132.9 2.0 collective-permute-start.34
  135.0 2.6 %collective-permute-done.35 = f32[1,1024]{1,0:T(1,128)S(1)} collective-permute-done((f32[1,1024]{1,0:T(1,128)S(1)}, f32[1,1024]{1,0:T(1,128)S(1)}, u32[]{:S(2)}, u32[]{:S(2)}) %collective-permute-start.35) | collective-permute-done | bytes 4128 | tf_op jit(solution)/shard_map/ppermute | solution.py:44
  137.6 2.1 collective-permute-done.33
  139.8 1.7 row_lse.3
  141.6 1.9 collective-permute-start.37
  143.7 3.0 %collective-permute-done.38 = f32[1,1024]{1,0:T(1,128)S(1)} collective-permute-done((f32[1,1024]{1,0:T(1,128)S(1)}, f32[1,1024]{1,0:T(1,128)S(1)}, u32[]{:S(2)}, u32[]{:S(2)}) %collective-permute-start.38) | collective-permute-done | bytes 4128 | tf_op jit(solution)/shard_map/ppermute | solution.py:44
  146.7 1.6 collective-permute-done.36
  148.4 1.5 collective-permute-start.40
  150.5 3.0 %collective-permute-done.41 = f32[1,1024]{1,0:T(1,128)S(1)} collective-permute-done((f32[1,1024]{1,0:T(1,128)S(1)}, f32[1,1024]{1,0:T(1,128)S(1)}, u32[]{:S(2)}, u32[]{:S(2)}) %collective-permute-start.41) | collective-permute-done | bytes 4128 | tf_op jit(solution)/shard_map/ppermute | solution.py:44
  155.3 1.6 col_lse.5
  158.4 1.5 collective-permute-start.44
  160.5 2.9 %collective-permute-done.45 = f32[1,1024]{1,0:T(1,128)S(1)} collective-permute-done((f32[1,1024]{1,0:T(1,128)S(1)}, f32[1,1024]{1,0:T(1,128)S(1)}, u32[]{:S(2)}, u32[]{:S(2)}) %collective-permute-start.45) | collective-permute-done | bytes 4128 | tf_op jit(solution)/shard_map/ppermute | solution.py:44
  165.4 5.1 %plan.1 = (bf16[1024,1024]{1,0:T(8,128)(2,1)S(1)}, f32[1,1024]{1,0:T(1,128)S(1)}, bf16[512,1024]{1,0:T(8,128)(2,1)S(1)}, bf16[512,1024]{1,0:T(8,128)(2,1)S(1)}) custom-call(s32[4]{0:T(128)S(1)} %pad_add_fusion.1.blocks_ref, f32[1024,1024]{1,0:T(8,128)S(1)} %get-tuple-element.10.logits_ref, f32[1,1024]{1,0:T(1,128)S(1)} %get-tuple-element.20.rowpot_ref, ...), custom_call_target="tpu_custom_call" | custom-call | flops 2147483648 | bytes 10485760 | tf_op jit(solution)/shard_map/plan/pallas_call | solution.py:387
  170.6 3.2 %collective-permute-start.50 = (bf16[512,1024]{1,0:T(8,128)(2,1)S(1)}, bf16[512,1024]{1,0:T(8,128)(2,1)S(1)}, u32[]{:S(2)}, u32[]{:S(2)}) collective-permute-start(bf16[512,1024]{1,0:T(8,128)(2,1)S(1)} %get-tuple-element.15), channel_id=1, source_target_pairs={{0,12},{1,13},{2,14},{3,15},{4,0},{5,1},{6,2},{7,3},{8,4},{9,5},{1... | collective-permute-start | bytes 3145736 | tf_op jit(solution)/shard_map/ppermute | solution.py:86
  173.9 2.8 %share.7 = bf16[512,1024]{1,0:T(8,128)(2,1)S(1)} custom-call(s32[4]{0:T(128)S(1)} %pad_add_fusion.3.blocks_ref, bf16[1024,1024]{1,0:T(8,128)(2,1)S(1)} %get-tuple-element.13.plan_ref, bf16[1024,4096]{1,0:T(8,128)(2,1)S(1)} %bitcast.29), custom_call_target="tpu_custom_call" | custom-call | flops 1073741824 | bytes 5242880 | tf_op jit(solution)/shard_map/share/pallas_call | solution.py:433
  177.0 9.6 %collective-permute-done.46.refs_0_ = bf16[512,1024]{1,0:T(8,128)(2,1)S(1)} collective-permute-done((bf16[512,1024]{1,0:T(8,128)(2,1)S(1)}, bf16[512,1024]{1,0:T(8,128)(2,1)S(1)}, u32[]{:S(2)}, u32[]{:S(2)}) %collective-permute-start.46) | collective-permute-done | bytes 1048608 | tf_op jit(solution)/shard_map/ppermute | solution.py:86
  186.6 2.9 %share.6 = bf16[512,1024]{1,0:T(8,128)(2,1)S(1)} custom-call(s32[4]{0:T(128)S(1)} %pad_add_fusion.2.blocks_ref, bf16[1024,1024]{1,0:T(8,128)(2,1)S(1)} %get-tuple-element.13.plan_ref, bf16[1024,4096]{1,0:T(8,128)(2,1)S(1)} %bitcast.29, bf16[512,1024]{1,0:T(8,128)(2,1)S(1)} %collective-permute-done.46.refs_0_), custom_call_target="tpu_custom_call" | custom-call | flops 1073741824 | bytes 5242880 | tf_op jit(solution)/shard_map/share/pallas_call | solution.py:433
  189.6 2.8 %share.8 = bf16[512,1024]{1,0:T(8,128)(2,1)S(1)} custom-call(s32[4]{0:T(128)S(1)} %pad_add_fusion.2.blocks_ref, bf16[1024,1024]{1,0:T(8,128)(2,1)S(1)} %get-tuple-element.13.plan_ref, bf16[1024,4096]{1,0:T(8,128)(2,1)S(1)} %bitcast.29), custom_call_target="tpu_custom_call" | custom-call | flops 1073741824 | bytes 5242880 | tf_op jit(solution)/shard_map/share/pallas_call | solution.py:433
  192.4 2.9 %share.9 = bf16[512,1024]{1,0:T(8,128)(2,1)S(1)} custom-call(s32[4]{0:T(128)S(1)} %pad_add_fusion.3.blocks_ref, bf16[1024,1024]{1,0:T(8,128)(2,1)S(1)} %get-tuple-element.13.plan_ref, bf16[1024,4096]{1,0:T(8,128)(2,1)S(1)} %bitcast.29, bf16[512,1024]{1,0:T(8,128)(2,1)S(1)} %collective-permute-done.50.refs_0_), custom_call_target="tpu_custom_call" | custom-call | flops 1073741824 | bytes 5242880 | tf_op jit(solution)/shard_map/share/pallas_call | solution.py:433
  195.3 3.3 %collective-permute-start.51 = (bf16[512,1024]{1,0:T(8,128)(2,1)S(1)}, bf16[512,1024]{1,0:T(8,128)(2,1)S(1)}, u32[]{:S(2)}, u32[]{:S(2)}) collective-permute-start(bf16[512,1024]{1,0:T(8,128)(2,1)S(1)} %share.9), channel_id=1, source_target_pairs={{0,12},{1,13},{2,14},{3,15},{4,0},{5,1},{6,2},{7,3},{8,4},{9,5},{1... | collective-permute-start | bytes 3145736 | tf_op jit(solution)/shard_map/ppermute | solution.py:86
  198.7 4.0 %share.5 = f32[1024,1024]{1,0:T(8,128)S(1)} custom-call(s32[4]{0:T(128)S(1)} %pad_add_fusion.blocks_ref, bf16[1024,1024]{1,0:T(8,128)(2,1)S(1)} %get-tuple-element.13.plan_ref, bf16[1024,4096]{1,0:T(8,128)(2,1)S(1)} %bitcast.29), custom_call_target="tpu_custom_call" | custom-call | flops 2147483648 | bytes 8388608 | tf_op jit(solution)/shard_map/share/pallas_call | solution.py:433
  202.8 2.8 %collective-permute-done.47 = bf16[512,1024]{1,0:T(8,128)(2,1)S(1)} collective-permute-done((bf16[512,1024]{1,0:T(8,128)(2,1)S(1)}, bf16[512,1024]{1,0:T(8,128)(2,1)S(1)}, u32[]{:S(2)}, u32[]{:S(2)}) %collective-permute-start.47) | collective-permute-done | bytes 1048608 | tf_op jit(solution)/shard_map/ppermute | solution.py:86
  205.9 10.9 %collective-permute-done.49 = bf16[512,1024]{1,0:T(8,128)(2,1)S(1)} collective-permute-done((bf16[512,1024]{1,0:T(8,128)(2,1)S(1)}, bf16[512,1024]{1,0:T(8,128)(2,1)S(1)}, u32[]{:S(2)}, u32[]{:S(2)}) %collective-permute-start.49) | collective-permute-done | bytes 1048608 | tf_op jit(solution)/shard_map/ppermute | solution.py:86
  220.0 3.1 %collective-permute-start.57 = (f32[1,1024]{1,0:T(1,128)S(1)}, f32[1,1024]{1,0:T(1,128)S(1)}, u32[]{:S(2)}, u32[]{:S(2)}) collective-permute-start(f32[1,1024]{1,0:T(1,128)S(1)} %get-tuple-element.16), channel_id=1, source_target_pairs={{0,2},{1,3},{2,0},{3,1},{4,6},{5,7},{6,4},{7,5},{8,10},{9,11},{10,... | collective-permute-start | bytes 12296 | tf_op jit(solution)/shard_map/ppermute | solution.py:44
  223.1 2.2 collective-permute-start.56
  225.3 7.6 %collective-permute-done.57 = f32[1,1024]{1,0:T(1,128)S(1)} collective-permute-done((f32[1,1024]{1,0:T(1,128)S(1)}, f32[1,1024]{1,0:T(1,128)S(1)}, u32[]{:S(2)}, u32[]{:S(2)}) %collective-permute-start.57) | collective-permute-done | bytes 4128 | tf_op jit(solution)/shard_map/ppermute | solution.py:44
  232.8 4.8 %collective-permute-done.55 = f32[1,1024]{1,0:T(1,128)S(1)} collective-permute-done((f32[1,1024]{1,0:T(1,128)S(1)}, f32[1,1024]{1,0:T(1,128)S(1)}, u32[]{:S(2)}, u32[]{:S(2)}) %collective-permute-start.55) | collective-permute-done | bytes 4128 | tf_op jit(solution)/shard_map/ppermute | solution.py:44
  237.7 1.5 collective-permute-start.59
  239.2 3.6 %collective-permute-done.60 = f32[1,1024]{1,0:T(1,128)S(1)} collective-permute-done((f32[1,1024]{1,0:T(1,128)S(1)}, f32[1,1024]{1,0:T(1,128)S(1)}, u32[]{:S(2)}, u32[]{:S(2)}) %collective-permute-start.60) | collective-permute-done | bytes 4128 | tf_op jit(solution)/shard_map/ppermute | solution.py:44
  242.9 4.8 %collective-permute-done.58 = f32[1,1024]{1,0:T(1,128)S(1)} collective-permute-done((f32[1,1024]{1,0:T(1,128)S(1)}, f32[1,1024]{1,0:T(1,128)S(1)}, u32[]{:S(2)}, u32[]{:S(2)}) %collective-permute-start.58) | collective-permute-done | bytes 4128 | tf_op jit(solution)/shard_map/ppermute | solution.py:44
  (122 shorter events, 35.6 us)
Async XLA Ops:
  0.6 11.5 %collective-permute-start.2 = (bf16[1024,256]{1,0:T(8,128)(2,1)}, bf16[1024,256]{1,0:T(8,128)(2,1)S(1)}, u32[]{:S(2)}, u32[]{:S(2)}) collective-permute-start(bf16[1024,256]{1,0:T(8,128)(2,1)} %refs_0_.1), channel_id=1, source_target_pairs={{0,2},{1,3},{2,0},{3,1},{4,6},{5,7},{6,4},{7,5},{8,10},{9,11},{10,... | collective-permute-start | bytes 1572872 | tf_op jit(solution)/shard_map/ppermute | solution.py:82
  4.7 14.0 %collective-permute-start.1 = (bf16[1024,256]{1,0:T(8,128)(2,1)}, bf16[1024,256]{1,0:T(8,128)(2,1)S(1)}, u32[]{:S(2)}, u32[]{:S(2)}) collective-permute-start(bf16[1024,256]{1,0:T(8,128)(2,1)} %refs_0_.1), channel_id=1, source_target_pairs={{0,3},{1,0},{2,1},{3,2},{4,7},{5,4},{6,5},{7,6},{8,11},{9,8},{10,9... | collective-permute-start | bytes 1572872 | tf_op jit(solution)/shard_map/ppermute | solution.py:82
  5.4 13.4 %collective-permute-start = (bf16[1024,256]{1,0:T(8,128)(2,1)}, bf16[1024,256]{1,0:T(8,128)(2,1)S(1)}, u32[]{:S(2)}, u32[]{:S(2)}) collective-permute-start(bf16[1024,256]{1,0:T(8,128)(2,1)} %refs_0_.1), channel_id=1, source_target_pairs={{0,1},{1,2},{2,3},{3,0},{4,5},{5,6},{6,7},{7,4},{8,9},{9,10},{10,1... | collective-permute-start | bytes 1572872 | tf_op jit(solution)/shard_map/ppermute | solution.py:82
  6.7 18.4 %collective-permute-start.9 = (bf16[1024,512]{1,0:T(8,128)(2,1)}, bf16[1024,512]{1,0:T(8,128)(2,1)S(1)}, u32[]{:S(2)}, u32[]{:S(2)}) collective-permute-start(bf16[1024,512]{1,0:T(8,128)(2,1)} %refs_10_.1), channel_id=1, source_target_pairs={{0,16},{16,0},{32,48},{48,32},{64,80},{80,64},{96,112},{112,96},{1... | collective-permute-start | bytes 3145736 | tf_op jit(solution)/shard_map/ppermute | solution.py:124
  6.7 18.4 %collective-permute-start.10 = (bf16[1024,512]{1,0:T(8,128)(2,1)}, bf16[1024,512]{1,0:T(8,128)(2,1)}, u32[]{:S(2)}, u32[]{:S(2)}) collective-permute-start(bf16[1024,512]{1,0:T(8,128)(2,1)} %refs_10_.1), channel_id=1, source_target_pairs={{0,32},{16,112},{32,64},{48,16},{64,96},{80,48},{96,0},{112,80},{1... | collective-permute-start | bytes 3145736 | tf_op jit(solution)/shard_map/ppermute | solution.py:125
  18.9 46.2 %copy-start = (bf16[1024,256]{1,0:T(8,128)(2,1)S(1)}, bf16[1024,256]{1,0:T(8,128)(2,1)}, u32[]{:S(2)}) copy-start(bf16[1024,256]{1,0:T(8,128)(2,1)} %refs_0_.1) | copy-start | bytes 1572868
  18.9 46.2 %copy-start.1 = (bf16[1024,512]{1,0:T(8,128)(2,1)S(1)}, bf16[1024,512]{1,0:T(8,128)(2,1)}, u32[]{:S(2)}) copy-start(bf16[1024,512]{1,0:T(8,128)(2,1)} %refs_10_.1) | copy-start | bytes 3145732
  18.9 15.1 %collective-permute-start.5 = (bf16[2048,256]{1,0:T(8,128)(2,1)S(1)}, bf16[2048,256]{1,0:T(8,128)(2,1)S(1)}, u32[]{:S(2)}, u32[]{:S(2)}) collective-permute-start(bf16[2048,256]{1,0:T(8,128)(2,1)S(1)} %pad_maximum_fusion), channel_id=1, source_target_pairs={{0,12},{1,13},{2,14},{3,15},{4,0},{5,1},{6,2},{7,3},{8,4},{9,5},{1... | collective-permute-start | bytes 3145736 | tf_op jit(solution)/shard_map/ppermute | solution.py:86
  21.7 16.1 %collective-permute-start.3 = (bf16[2048,256]{1,0:T(8,128)(2,1)S(1)}, bf16[2048,256]{1,0:T(8,128)(2,1)}, u32[]{:S(2)}, u32[]{:S(2)}) collective-permute-start(bf16[2048,256]{1,0:T(8,128)(2,1)S(1)} %pad_maximum_fusion), channel_id=1, source_target_pairs={{0,4},{1,5},{2,6},{3,7},{4,8},{5,9},{6,10},{7,11},{8,12},{9,13},{1... | collective-permute-start | bytes 3145736 | tf_op jit(solution)/shard_map/ppermute | solution.py:86
  21.8 23.5 %collective-permute-start.6 = (bf16[2048,256]{1,0:T(8,128)(2,1)S(1)}, bf16[2048,256]{1,0:T(8,128)(2,1)}, u32[]{:S(2)}, u32[]{:S(2)}) collective-permute-start(bf16[2048,256]{1,0:T(8,128)(2,1)S(1)} %pad_maximum_fusion.1), channel_id=1, source_target_pairs={{0,12},{1,13},{2,14},{3,15},{4,0},{5,1},{6,2},{7,3},{8,4},{9,5},{1... | collective-permute-start | bytes 3145736 | tf_op jit(solution)/shard_map/ppermute | solution.py:86
  25.1 23.9 %collective-permute-start.4 = (bf16[2048,256]{1,0:T(8,128)(2,1)S(1)}, bf16[2048,256]{1,0:T(8,128)(2,1)S(1)}, u32[]{:S(2)}, u32[]{:S(2)}) collective-permute-start(bf16[2048,256]{1,0:T(8,128)(2,1)S(1)} %pad_maximum_fusion.1), channel_id=1, source_target_pairs={{0,4},{1,5},{2,6},{3,7},{4,8},{5,9},{6,10},{7,11},{8,12},{9,13},{1... | collective-permute-start | bytes 3145736 | tf_op jit(solution)/shard_map/ppermute | solution.py:86
  25.1 25.0 %collective-permute-start.11 = (bf16[1024,512]{1,0:T(8,128)(2,1)S(1)}, bf16[1024,512]{1,0:T(8,128)(2,1)}, u32[]{:S(2)}, u32[]{:S(2)}) collective-permute-start(bf16[1024,512]{1,0:T(8,128)(2,1)S(1)} %collective-permute-done.9.refs_11_), channel_id=1, source_target_pairs={{0,32},{16,112},{32,64},{48,16},{64,96},{80,48},{96,0},{112,80},{1... | collective-permute-start | bytes 3145736 | tf_op jit(solution)/shard_map/ppermute | solution.py:125
  35.1 17.5 %collective-permute-start.12 = (bf16[1024,512]{1,0:T(8,128)(2,1)}, bf16[1024,512]{1,0:T(8,128)(2,1)}, u32[]{:S(2)}, u32[]{:S(2)}) collective-permute-start(bf16[1024,512]{1,0:T(8,128)(2,1)} %collective-permute-done.10.refs_12_), channel_id=1, source_target_pairs={{0,32},{16,112},{32,64},{48,16},{64,96},{80,48},{96,0},{112,80},{1... | collective-permute-start | bytes 3145736 | tf_op jit(solution)/shard_map/ppermute | solution.py:125
  37.9 14.8 %collective-permute-start.13 = (bf16[1024,512]{1,0:T(8,128)(2,1)}, bf16[1024,512]{1,0:T(8,128)(2,1)}, u32[]{:S(2)}, u32[]{:S(2)}) collective-permute-start(bf16[1024,512]{1,0:T(8,128)(2,1)} %collective-permute-done.10.refs_12_), channel_id=1, source_target_pairs={{0,16},{16,0},{32,48},{48,32},{64,80},{80,64},{96,112},{112,96},{1... | collective-permute-start | bytes 3145736 | tf_op jit(solution)/shard_map/ppermute | solution.py:124
  45.3 16.9 %collective-permute-start.7 = (bf16[2048,256]{1,0:T(8,128)(2,1)}, bf16[2048,256]{1,0:T(8,128)(2,1)}, u32[]{:S(2)}, u32[]{:S(2)}) collective-permute-start(bf16[2048,256]{1,0:T(8,128)(2,1)} %collective-permute-done.3.refs_4_), channel_id=1, source_target_pairs={{0,4},{1,5},{2,6},{3,7},{4,8},{5,9},{6,10},{7,11},{8,12},{9,13},{1... | collective-permute-start | bytes 3145736 | tf_op jit(solution)/shard_map/ppermute | solution.py:86
  50.0 15.1 %collective-permute-start.8 = (bf16[2048,256]{1,0:T(8,128)(2,1)}, bf16[2048,256]{1,0:T(8,128)(2,1)}, u32[]{:S(2)}, u32[]{:S(2)}) collective-permute-start(bf16[2048,256]{1,0:T(8,128)(2,1)} %collective-permute-done.6.refs_7_), channel_id=1, source_target_pairs={{0,12},{1,13},{2,14},{3,15},{4,0},{5,1},{6,2},{7,3},{8,4},{9,5},{1... | collective-permute-start | bytes 3145736 | tf_op jit(solution)/shard_map/ppermute | solution.py:86
  50.1 15.0 %collective-permute-start.14 = (bf16[1024,512]{1,0:T(8,128)(2,1)}, bf16[1024,512]{1,0:T(8,128)(2,1)}, u32[]{:S(2)}, u32[]{:S(2)}) collective-permute-start(bf16[1024,512]{1,0:T(8,128)(2,1)} %collective-permute-done.11.refs_13_), channel_id=1, source_target_pairs={{0,16},{16,0},{32,48},{48,32},{64,80},{80,64},{96,112},{112,96},{1... | collective-permute-start | bytes 3145736 | tf_op jit(solution)/shard_map/ppermute | solution.py:124
  52.5 12.6 %collective-permute-start.15 = (bf16[1024,512]{1,0:T(8,128)(2,1)}, bf16[1024,512]{1,0:T(8,128)(2,1)}, u32[]{:S(2)}, u32[]{:S(2)}) collective-permute-start(bf16[1024,512]{1,0:T(8,128)(2,1)} %collective-permute-done.12.refs_14_), channel_id=1, source_target_pairs={{0,16},{16,0},{32,48},{48,32},{64,80},{80,64},{96,112},{112,96},{1... | collective-permute-start | bytes 3145736 | tf_op jit(solution)/shard_map/ppermute | solution.py:124
  84.7 5.4 %collective-permute-start.18 = (f32[1,1024]{1,0:T(1,128)S(1)}, f32[1,1024]{1,0:T(1,128)S(1)}, u32[]{:S(2)}, u32[]{:S(2)}) collective-permute-start(f32[1,1024]{1,0:T(1,128)S(1)} %get-tuple-element.11), channel_id=1, source_target_pairs={{0,2},{1,3},{2,0},{3,1},{4,6},{5,7},{6,4},{7,5},{8,10},{9,11},{10,... | collective-permute-start | bytes 12296 | tf_op jit(solution)/shard_map/ppermute | solution.py:44
  87.3 3.6 %collective-permute-start.17 = (f32[1,1024]{1,0:T(1,128)S(1)}, f32[1,1024]{1,0:T(1,128)S(1)}, u32[]{:S(2)}, u32[]{:S(2)}) collective-permute-start(f32[1,1024]{1,0:T(1,128)S(1)} %get-tuple-element.11), channel_id=1, source_target_pairs={{0,3},{1,0},{2,1},{3,2},{4,7},{5,4},{6,5},{7,6},{8,11},{9,8},{10,9... | collective-permute-start | bytes 12296 | tf_op jit(solution)/shard_map/ppermute | solution.py:44
  88.5 4.8 %collective-permute-start.16 = (f32[1,1024]{1,0:T(1,128)S(1)}, f32[1,1024]{1,0:T(1,128)S(1)}, u32[]{:S(2)}, u32[]{:S(2)}) collective-permute-start(f32[1,1024]{1,0:T(1,128)S(1)} %get-tuple-element.11), channel_id=1, source_target_pairs={{0,1},{1,2},{2,3},{3,0},{4,5},{5,6},{6,7},{7,4},{8,9},{9,10},{10,1... | collective-permute-start | bytes 12296 | tf_op jit(solution)/shard_map/ppermute | solution.py:44
  93.4 5.2 %collective-permute-start.21 = (f32[1,1024]{1,0:T(1,128)S(1)}, f32[1,1024]{1,0:T(1,128)S(1)}, u32[]{:S(2)}, u32[]{:S(2)}) collective-permute-start(f32[1,1024]{1,0:T(1,128)S(1)} %multiply_add_fusion.5), channel_id=1, source_target_pairs={{0,8},{1,9},{2,10},{3,11},{4,12},{5,13},{6,14},{7,15},{8,0},{9,1},... | collective-permute-start | bytes 12296 | tf_op jit(solution)/shard_map/ppermute | solution.py:44
  95.1 3.6 %collective-permute-start.20 = (f32[1,1024]{1,0:T(1,128)S(1)}, f32[1,1024]{1,0:T(1,128)S(1)}, u32[]{:S(2)}, u32[]{:S(2)}) collective-permute-start(f32[1,1024]{1,0:T(1,128)S(1)} %multiply_add_fusion.5), channel_id=1, source_target_pairs={{0,12},{1,13},{2,14},{3,15},{4,0},{5,1},{6,2},{7,3},{8,4},{9,5},{1... | collective-permute-start | bytes 12296 | tf_op jit(solution)/shard_map/ppermute | solution.py:44
  95.7 4.8 %collective-permute-start.19 = (f32[1,1024]{1,0:T(1,128)S(1)}, f32[1,1024]{1,0:T(1,128)S(1)}, u32[]{:S(2)}, u32[]{:S(2)}) collective-permute-start(f32[1,1024]{1,0:T(1,128)S(1)} %multiply_add_fusion.5), channel_id=1, source_target_pairs={{0,4},{1,5},{2,6},{3,7},{4,8},{5,9},{6,10},{7,11},{8,12},{9,13},{1... | collective-permute-start | bytes 12296 | tf_op jit(solution)/shard_map/ppermute | solution.py:44
  102.2 1.2 collective-permute-start.22
  103.5 5.3 %collective-permute-start.25 = (f32[1,1024]{1,0:T(1,128)S(1)}, f32[1,1024]{1,0:T(1,128)S(1)}, u32[]{:S(2)}, u32[]{:S(2)}) collective-permute-start(f32[1,1024]{1,0:T(1,128)S(1)} %multiply_add_fusion.4), channel_id=1, source_target_pairs={{0,64},{16,80},{32,96},{48,112},{64,0},{80,16},{96,32},{112,48},{1... | collective-permute-start | bytes 12296 | tf_op jit(solution)/shard_map/ppermute | solution.py:44
  106.8 3.6 %collective-permute-start.24 = (f32[1,1024]{1,0:T(1,128)S(1)}, f32[1,1024]{1,0:T(1,128)S(1)}, u32[]{:S(2)}, u32[]{:S(2)}) collective-permute-start(f32[1,1024]{1,0:T(1,128)S(1)} %multiply_add_fusion.4), channel_id=1, source_target_pairs={{0,96},{16,112},{32,0},{48,16},{64,32},{80,48},{96,64},{112,80},{1... | collective-permute-start | bytes 12296 | tf_op jit(solution)/shard_map/ppermute | solution.py:44
  107.8 4.8 %collective-permute-start.23 = (f32[1,1024]{1,0:T(1,128)S(1)}, f32[1,1024]{1,0:T(1,128)S(1)}, u32[]{:S(2)}, u32[]{:S(2)}) collective-permute-start(f32[1,1024]{1,0:T(1,128)S(1)} %multiply_add_fusion.4), channel_id=1, source_target_pairs={{0,32},{16,48},{32,64},{48,80},{64,96},{80,112},{96,0},{112,16},{1... | collective-permute-start | bytes 12296 | tf_op jit(solution)/shard_map/ppermute | solution.py:44
  112.7 52.6 %slice-start = ((s8[8388608]{0:T(1024)(128)(4,1)}), s8[4194304]{0:T(1024)(128)(4,1)S(1)}, s32[]{:S(2)}) async-start(s8[8388608]{0:T(1024)(128)(4,1)} %bitcast.28), calls=%async_computation | async-start | bytes 8388608
  114.4 5.2 %collective-permute-start.28 = (f32[1,1024]{1,0:T(1,128)S(1)}, f32[1,1024]{1,0:T(1,128)S(1)}, u32[]{:S(2)}, u32[]{:S(2)}) collective-permute-start(f32[1,1024]{1,0:T(1,128)S(1)} %row_lse.2), channel_id=1, source_target_pairs={{0,2},{1,3},{2,0},{3,1},{4,6},{5,7},{6,4},{7,5},{8,10},{9,11},{10,... | collective-permute-start | bytes 12296 | tf_op jit(solution)/shard_map/ppermute | solution.py:44
  115.2 4.4 %collective-permute-start.27 = (f32[1,1024]{1,0:T(1,128)S(1)}, f32[1,1024]{1,0:T(1,128)S(1)}, u32[]{:S(2)}, u32[]{:S(2)}) collective-permute-start(f32[1,1024]{1,0:T(1,128)S(1)} %row_lse.2), channel_id=1, source_target_pairs={{0,3},{1,0},{2,1},{3,2},{4,7},{5,4},{6,5},{7,6},{8,11},{9,8},{10,9... | collective-permute-start | bytes 12296 | tf_op jit(solution)/shard_map/ppermute | solution.py:44
  116.8 4.8 %collective-permute-start.26 = (f32[1,1024]{1,0:T(1,128)S(1)}, f32[1,1024]{1,0:T(1,128)S(1)}, u32[]{:S(2)}, u32[]{:S(2)}) collective-permute-start(f32[1,1024]{1,0:T(1,128)S(1)} %row_lse.2), channel_id=1, source_target_pairs={{0,1},{1,2},{2,3},{3,0},{4,5},{5,6},{6,7},{7,4},{8,9},{9,10},{10,1... | collective-permute-start | bytes 12296 | tf_op jit(solution)/shard_map/ppermute | solution.py:44
  121.6 5.2 %collective-permute-start.31 = (f32[1,1024]{1,0:T(1,128)S(1)}, f32[1,1024]{1,0:T(1,128)S(1)}, u32[]{:S(2)}, u32[]{:S(2)}) collective-permute-start(f32[1,1024]{1,0:T(1,128)S(1)} %multiply_add_fusion.3), channel_id=1, source_target_pairs={{0,8},{1,9},{2,10},{3,11},{4,12},{5,13},{6,14},{7,15},{8,0},{9,1},... | collective-permute-start | bytes 12296 | tf_op jit(solution)/shard_map/ppermute | solution.py:44
  122.5 4.3 %collective-permute-start.30 = (f32[1,1024]{1,0:T(1,128)S(1)}, f32[1,1024]{1,0:T(1,128)S(1)}, u32[]{:S(2)}, u32[]{:S(2)}) collective-permute-start(f32[1,1024]{1,0:T(1,128)S(1)} %multiply_add_fusion.3), channel_id=1, source_target_pairs={{0,12},{1,13},{2,14},{3,15},{4,0},{5,1},{6,2},{7,3},{8,4},{9,5},{1... | collective-permute-start | bytes 12296 | tf_op jit(solution)/shard_map/ppermute | solution.py:44
  124.6 4.8 %collective-permute-start.29 = (f32[1,1024]{1,0:T(1,128)S(1)}, f32[1,1024]{1,0:T(1,128)S(1)}, u32[]{:S(2)}, u32[]{:S(2)}) collective-permute-start(f32[1,1024]{1,0:T(1,128)S(1)} %multiply_add_fusion.3), channel_id=1, source_target_pairs={{0,4},{1,5},{2,6},{3,7},{4,8},{5,9},{6,10},{7,11},{8,12},{9,13},{1... | collective-permute-start | bytes 12296 | tf_op jit(solution)/shard_map/ppermute | solution.py:44
  131.1 1.2 collective-permute-start.32
  132.4 5.2 %collective-permute-start.35 = (f32[1,1024]{1,0:T(1,128)S(1)}, f32[1,1024]{1,0:T(1,128)S(1)}, u32[]{:S(2)}, u32[]{:S(2)}) collective-permute-start(f32[1,1024]{1,0:T(1,128)S(1)} %multiply_add_fusion.2), channel_id=1, source_target_pairs={{0,64},{16,80},{32,96},{48,112},{64,0},{80,16},{96,32},{112,48},{1... | collective-permute-start | bytes 12296 | tf_op jit(solution)/shard_map/ppermute | solution.py:44
  132.9 4.6 %collective-permute-start.34 = (f32[1,1024]{1,0:T(1,128)S(1)}, f32[1,1024]{1,0:T(1,128)S(1)}, u32[]{:S(2)}, u32[]{:S(2)}) collective-permute-start(f32[1,1024]{1,0:T(1,128)S(1)} %multiply_add_fusion.2), channel_id=1, source_target_pairs={{0,96},{16,112},{32,0},{48,16},{64,32},{80,48},{96,64},{112,80},{1... | collective-permute-start | bytes 12296 | tf_op jit(solution)/shard_map/ppermute | solution.py:44
  134.9 4.8 %collective-permute-start.33 = (f32[1,1024]{1,0:T(1,128)S(1)}, f32[1,1024]{1,0:T(1,128)S(1)}, u32[]{:S(2)}, u32[]{:S(2)}) collective-permute-start(f32[1,1024]{1,0:T(1,128)S(1)} %multiply_add_fusion.2), channel_id=1, source_target_pairs={{0,32},{16,48},{32,64},{48,80},{64,96},{80,112},{96,0},{112,16},{1... | collective-permute-start | bytes 12296 | tf_op jit(solution)/shard_map/ppermute | solution.py:44
  141.5 5.2 %collective-permute-start.38 = (f32[1,1024]{1,0:T(1,128)S(1)}, f32[1,1024]{1,0:T(1,128)S(1)}, u32[]{:S(2)}, u32[]{:S(2)}) collective-permute-start(f32[1,1024]{1,0:T(1,128)S(1)} %row_lse.3), channel_id=1, source_target_pairs={{0,2},{1,3},{2,0},{3,1},{4,6},{5,7},{6,4},{7,5},{8,10},{9,11},{10,... | collective-permute-start | bytes 12296 | tf_op jit(solution)/shard_map/ppermute | solution.py:44
  141.6 5.1 %collective-permute-start.37 = (f32[1,1024]{1,0:T(1,128)S(1)}, f32[1,1024]{1,0:T(1,128)S(1)}, u32[]{:S(2)}, u32[]{:S(2)}) collective-permute-start(f32[1,1024]{1,0:T(1,128)S(1)} %row_lse.3), channel_id=1, source_target_pairs={{0,3},{1,0},{2,1},{3,2},{4,7},{5,4},{6,5},{7,6},{8,11},{9,8},{10,9... | collective-permute-start | bytes 12296 | tf_op jit(solution)/shard_map/ppermute | solution.py:44
  143.5 4.8 %collective-permute-start.36 = (f32[1,1024]{1,0:T(1,128)S(1)}, f32[1,1024]{1,0:T(1,128)S(1)}, u32[]{:S(2)}, u32[]{:S(2)}) collective-permute-start(f32[1,1024]{1,0:T(1,128)S(1)} %row_lse.3), channel_id=1, source_target_pairs={{0,1},{1,2},{2,3},{3,0},{4,5},{5,6},{6,7},{7,4},{8,9},{9,10},{10,1... | collective-permute-start | bytes 12296 | tf_op jit(solution)/shard_map/ppermute | solution.py:44
  148.3 5.2 %collective-permute-start.41 = (f32[1,1024]{1,0:T(1,128)S(1)}, f32[1,1024]{1,0:T(1,128)S(1)}, u32[]{:S(2)}, u32[]{:S(2)}) collective-permute-start(f32[1,1024]{1,0:T(1,128)S(1)} %multiply_add_fusion.1), channel_id=1, source_target_pairs={{0,8},{1,9},{2,10},{3,11},{4,12},{5,13},{6,14},{7,15},{8,0},{9,1},... | collective-permute-start | bytes 12296 | tf_op jit(solution)/shard_map/ppermute | solution.py:44
  148.4 5.1 %collective-permute-start.40 = (f32[1,1024]{1,0:T(1,128)S(1)}, f32[1,1024]{1,0:T(1,128)S(1)}, u32[]{:S(2)}, u32[]{:S(2)}) collective-permute-start(f32[1,1024]{1,0:T(1,128)S(1)} %multiply_add_fusion.1), channel_id=1, source_target_pairs={{0,12},{1,13},{2,14},{3,15},{4,0},{5,1},{6,2},{7,3},{8,4},{9,5},{1... | collective-permute-start | bytes 12296 | tf_op jit(solution)/shard_map/ppermute | solution.py:44
  149.9 4.8 %collective-permute-start.39 = (f32[1,1024]{1,0:T(1,128)S(1)}, f32[1,1024]{1,0:T(1,128)S(1)}, u32[]{:S(2)}, u32[]{:S(2)}) collective-permute-start(f32[1,1024]{1,0:T(1,128)S(1)} %multiply_add_fusion.1), channel_id=1, source_target_pairs={{0,4},{1,5},{2,6},{3,7},{4,8},{5,9},{6,10},{7,11},{8,12},{9,13},{1... | collective-permute-start | bytes 12296 | tf_op jit(solution)/shard_map/ppermute | solution.py:44
  157.0 1.2 collective-permute-start.42
  158.3 5.2 %collective-permute-start.45 = (f32[1,1024]{1,0:T(1,128)S(1)}, f32[1,1024]{1,0:T(1,128)S(1)}, u32[]{:S(2)}, u32[]{:S(2)}) collective-permute-start(f32[1,1024]{1,0:T(1,128)S(1)} %multiply_add_fusion), channel_id=1, source_target_pairs={{0,64},{16,80},{32,96},{48,112},{64,0},{80,16},{96,32},{112,48},{1... | collective-permute-start | bytes 12296 | tf_op jit(solution)/shard_map/ppermute | solution.py:44
  158.4 5.1 %collective-permute-start.44 = (f32[1,1024]{1,0:T(1,128)S(1)}, f32[1,1024]{1,0:T(1,128)S(1)}, u32[]{:S(2)}, u32[]{:S(2)}) collective-permute-start(f32[1,1024]{1,0:T(1,128)S(1)} %multiply_add_fusion), channel_id=1, source_target_pairs={{0,96},{16,112},{32,0},{48,16},{64,32},{80,48},{96,64},{112,80},{1... | collective-permute-start | bytes 12296 | tf_op jit(solution)/shard_map/ppermute | solution.py:44
  159.9 4.8 %collective-permute-start.43 = (f32[1,1024]{1,0:T(1,128)S(1)}, f32[1,1024]{1,0:T(1,128)S(1)}, u32[]{:S(2)}, u32[]{:S(2)}) collective-permute-start(f32[1,1024]{1,0:T(1,128)S(1)} %multiply_add_fusion), channel_id=1, source_target_pairs={{0,32},{16,48},{32,64},{48,80},{64,96},{80,112},{96,0},{112,16},{1... | collective-permute-start | bytes 12296 | tf_op jit(solution)/shard_map/ppermute | solution.py:44
  170.5 16.1 %collective-permute-start.46 = (bf16[512,1024]{1,0:T(8,128)(2,1)S(1)}, bf16[512,1024]{1,0:T(8,128)(2,1)S(1)}, u32[]{:S(2)}, u32[]{:S(2)}) collective-permute-start(bf16[512,1024]{1,0:T(8,128)(2,1)S(1)} %get-tuple-element.14), channel_id=1, source_target_pairs={{0,4},{1,5},{2,6},{3,7},{4,8},{5,9},{6,10},{7,11},{8,12},{9,13},{1... | collective-permute-start | bytes 3145736 | tf_op jit(solution)/shard_map/ppermute | solution.py:86
  170.6 21.9 %collective-permute-start.50 = (bf16[512,1024]{1,0:T(8,128)(2,1)S(1)}, bf16[512,1024]{1,0:T(8,128)(2,1)S(1)}, u32[]{:S(2)}, u32[]{:S(2)}) collective-permute-start(bf16[512,1024]{1,0:T(8,128)(2,1)S(1)} %get-tuple-element.15), channel_id=1, source_target_pairs={{0,12},{1,13},{2,14},{3,15},{4,0},{5,1},{6,2},{7,3},{8,4},{9,5},{1... | collective-permute-start | bytes 3145736 | tf_op jit(solution)/shard_map/ppermute | solution.py:86
  176.7 26.0 %collective-permute-start.48 = (bf16[512,1024]{1,0:T(8,128)(2,1)S(1)}, bf16[512,1024]{1,0:T(8,128)(2,1)S(1)}, u32[]{:S(2)}, u32[]{:S(2)}) collective-permute-start(bf16[512,1024]{1,0:T(8,128)(2,1)S(1)} %share.7), channel_id=1, source_target_pairs={{0,12},{1,13},{2,14},{3,15},{4,0},{5,1},{6,2},{7,3},{8,4},{9,5},{1... | collective-permute-start | bytes 3145736 | tf_op jit(solution)/shard_map/ppermute | solution.py:86
  189.5 16.1 %collective-permute-start.47 = (bf16[512,1024]{1,0:T(8,128)(2,1)S(1)}, bf16[512,1024]{1,0:T(8,128)(2,1)S(1)}, u32[]{:S(2)}, u32[]{:S(2)}) collective-permute-start(bf16[512,1024]{1,0:T(8,128)(2,1)S(1)} %share.6), channel_id=1, source_target_pairs={{0,4},{1,5},{2,6},{3,7},{4,8},{5,9},{6,10},{7,11},{8,12},{9,13},{1... | collective-permute-start | bytes 3145736 | tf_op jit(solution)/shard_map/ppermute | solution.py:86
  192.3 24.5 %collective-permute-start.49 = (bf16[512,1024]{1,0:T(8,128)(2,1)S(1)}, bf16[512,1024]{1,0:T(8,128)(2,1)S(1)}, u32[]{:S(2)}, u32[]{:S(2)}) collective-permute-start(bf16[512,1024]{1,0:T(8,128)(2,1)S(1)} %share.8), channel_id=1, source_target_pairs={{0,4},{1,5},{2,6},{3,7},{4,8},{5,9},{6,10},{7,11},{8,12},{9,13},{1... | collective-permute-start | bytes 3145736 | tf_op jit(solution)/shard_map/ppermute | solution.py:86
  195.3 21.5 %collective-permute-start.51 = (bf16[512,1024]{1,0:T(8,128)(2,1)S(1)}, bf16[512,1024]{1,0:T(8,128)(2,1)S(1)}, u32[]{:S(2)}, u32[]{:S(2)}) collective-permute-start(bf16[512,1024]{1,0:T(8,128)(2,1)S(1)} %share.9), channel_id=1, source_target_pairs={{0,12},{1,13},{2,14},{3,15},{4,0},{5,1},{6,2},{7,3},{8,4},{9,5},{1... | collective-permute-start | bytes 3145736 | tf_op jit(solution)/shard_map/ppermute | solution.py:86
  217.2 30.4 %collective-permute-start.52 = (bf16[1024,256]{1,0:T(8,128)(2,1)S(1)}, bf16[1024,256]{1,0:T(8,128)(2,1)S(1)}, u32[]{:S(2)}, u32[]{:S(2)}) collective-permute-start(bf16[1024,256]{1,0:T(8,128)(2,1)S(1)} %pad_maximum_fusion.2), channel_id=1, source_target_pairs={{0,3},{1,0},{2,1},{3,2},{4,7},{5,4},{6,5},{7,6},{8,11},{9,8},{10,9... | collective-permute-start | bytes 1572872 | tf_op jit(solution)/shard_map/ppermute | solution.py:82
  218.3 29.4 %collective-permute-start.53 = (bf16[1024,256]{1,0:T(8,128)(2,1)S(1)}, bf16[1024,256]{1,0:T(8,128)(2,1)S(1)}, u32[]{:S(2)}, u32[]{:S(2)}) collective-permute-start(bf16[1024,256]{1,0:T(8,128)(2,1)S(1)} %pad_maximum_fusion.3), channel_id=1, source_target_pairs={{0,1},{1,2},{2,3},{3,0},{4,5},{5,6},{6,7},{7,4},{8,9},{9,10},{10,1... | collective-permute-start | bytes 1572872 | tf_op jit(solution)/shard_map/ppermute | solution.py:82
  219.5 28.2 %collective-permute-start.54 = (bf16[1024,256]{1,0:T(8,128)(2,1)S(1)}, bf16[1024,256]{1,0:T(8,128)(2,1)S(1)}, u32[]{:S(2)}, u32[]{:S(2)}) collective-permute-start(bf16[1024,256]{1,0:T(8,128)(2,1)S(1)} %pad_maximum_fusion.4), channel_id=1, source_target_pairs={{0,2},{1,3},{2,0},{3,1},{4,6},{5,7},{6,4},{7,5},{8,10},{9,11},{10,... | collective-permute-start | bytes 1572872 | tf_op jit(solution)/shard_map/ppermute | solution.py:82
  220.0 12.9 %collective-permute-start.57 = (f32[1,1024]{1,0:T(1,128)S(1)}, f32[1,1024]{1,0:T(1,128)S(1)}, u32[]{:S(2)}, u32[]{:S(2)}) collective-permute-start(f32[1,1024]{1,0:T(1,128)S(1)} %get-tuple-element.16), channel_id=1, source_target_pairs={{0,2},{1,3},{2,0},{3,1},{4,6},{5,7},{6,4},{7,5},{8,10},{9,11},{10,... | collective-permute-start | bytes 12296 | tf_op jit(solution)/shard_map/ppermute | solution.py:44
  223.1 9.7 %collective-permute-start.56 = (f32[1,1024]{1,0:T(1,128)S(1)}, f32[1,1024]{1,0:T(1,128)S(1)}, u32[]{:S(2)}, u32[]{:S(2)}) collective-permute-start(f32[1,1024]{1,0:T(1,128)S(1)} %get-tuple-element.16), channel_id=1, source_target_pairs={{0,3},{1,0},{2,1},{3,2},{4,7},{5,4},{6,5},{7,6},{8,11},{9,8},{10,9... | collective-permute-start | bytes 12296 | tf_op jit(solution)/shard_map/ppermute | solution.py:44
  232.8 4.8 %collective-permute-start.55 = (f32[1,1024]{1,0:T(1,128)S(1)}, f32[1,1024]{1,0:T(1,128)S(1)}, u32[]{:S(2)}, u32[]{:S(2)}) collective-permute-start(f32[1,1024]{1,0:T(1,128)S(1)} %get-tuple-element.16), channel_id=1, source_target_pairs={{0,1},{1,2},{2,3},{3,0},{4,5},{5,6},{6,7},{7,4},{8,9},{9,10},{10,1... | collective-permute-start | bytes 12296 | tf_op jit(solution)/shard_map/ppermute | solution.py:44
  237.7 5.2 %collective-permute-start.60 = (f32[1,1024]{1,0:T(1,128)S(1)}, f32[1,1024]{1,0:T(1,128)S(1)}, u32[]{:S(2)}, u32[]{:S(2)}) collective-permute-start(f32[1,1024]{1,0:T(1,128)S(1)} %add_add_fusion.1), channel_id=1, source_target_pairs={{0,8},{1,9},{2,10},{3,11},{4,12},{5,13},{6,14},{7,15},{8,0},{9,1},... | collective-permute-start | bytes 12296 | tf_op jit(solution)/shard_map/ppermute | solution.py:44
  237.7 5.1 %collective-permute-start.59 = (f32[1,1024]{1,0:T(1,128)S(1)}, f32[1,1024]{1,0:T(1,128)S(1)}, u32[]{:S(2)}, u32[]{:S(2)}) collective-permute-start(f32[1,1024]{1,0:T(1,128)S(1)} %add_add_fusion.1), channel_id=1, source_target_pairs={{0,12},{1,13},{2,14},{3,15},{4,0},{5,1},{6,2},{7,3},{8,4},{9,5},{1... | collective-permute-start | bytes 12296 | tf_op jit(solution)/shard_map/ppermute | solution.py:44
  242.8 4.8 %collective-permute-start.58 = (f32[1,1024]{1,0:T(1,128)S(1)}, f32[1,1024]{1,0:T(1,128)S(1)}, u32[]{:S(2)}, u32[]{:S(2)}) collective-permute-start(f32[1,1024]{1,0:T(1,128)S(1)} %add_add_fusion.1), channel_id=1, source_target_pairs={{0,4},{1,5},{2,6},{3,7},{4,8},{5,9},{6,10},{7,11},{8,12},{9,13},{1... | collective-permute-start | bytes 12296 | tf_op jit(solution)/shard_map/ppermute | solution.py:44
  (7 other events, 32.2 us)
